TPU v7x, 256 devices: a whole 4x4x8 slice. The times are simulated.
256 devices in a mesh: block: 8 (over x_lo, y), tile: 32 (over z, x_hi, core).
Axes of the slice: x: 4 (x_hi: 2, x_lo: 2; x = x_hi * 2 + x_lo), y: 4, z: 8, core: 2. Of those that a mesh axis runs over, the one named last changes fastest.
Arguments:
- inputs: bfloat16 [32, 64, 96, 256], P('block', 'tile'), may hold values from -600 to 600
- out_grads: bfloat16 [32, 64, 96, 256], P('block', 'tile'), may hold values from -150 to 150
- kernel: bfloat16 [3, 3, 96, 3, 96], replicated, may hold values from -0.125 to 0.125
- norm_gain: float32 [96], replicated, may hold values from 0.1 to 1.9
- norm_shift: float32 [96], replicated, may hold values from -3 to 3
Outputs:
- input_grad: bfloat16 [32, 64, 96, 256], P('block', 'tile')
- kernel_grad: float32 [3, 3, 96, 3, 96], replicated
- gain_grad: float32 [96], replicated
- shift_grad: float32 [96], replicated
All inputs are finite; a program needn't handle non-finite values.
Results may differ from a plain program's by a relative error of at most 0.006.
Values may be sent and summed in bfloat16 or wider, within the bound.
A program may use at most 64 MiB of HBM per device.

v0:
```python
import jax
import jax.numpy as jnp
from jax import lax
from jax.sharding import PartitionSpec as P

GROUPS = 32


loss_scale = 1024.0
epsilon = 1e-06


def passed_along(block, axis, distance):
    devices = range(lax.axis_size(axis))
    route = [(i - distance, i) for i in devices if i - distance in devices]
    return lax.ppermute(block, axis, route)


def extended(block, sides, width):
    for axis, dim in sides:
        count = lax.axis_size(axis)
        forward = [(i, i + 1) for i in range(count - 1)]
        backward = [(target, source) for source, target in forward]
        low = lax.ppermute(
            lax.slice_in_dim(block, block.shape[dim] - width, None, axis=dim), axis, forward
        )
        high = lax.ppermute(lax.slice_in_dim(block, 0, width, axis=dim), axis, backward)
        block = jnp.concatenate([low, block, high], axis=dim)
    return block


def activate(values, center, spread, norm_gain, norm_shift):
    frame_count, row_count, channels, columns = values.shape
    grouped = values.astype(jnp.float32).reshape(
        frame_count, row_count, GROUPS, channels // GROUPS, columns
    )
    normed = ((grouped - center[:, None, :, None, None]) * spread[:, None, :, None, None]).reshape(
        frame_count, row_count, channels, columns
    )
    shaped = normed * norm_gain[None, None, :, None] + norm_shift[None, None, :, None]
    return (normed, shaped)


def kernel_terms(out_grads, padded):
    frame_count, row_count, channels, columns = out_grads.shape
    partials = []
    for time_tap in range(3):
        for row_tap in range(3):
            stacked = jnp.concatenate(
                [
                    padded[
                        time_tap : time_tap + frame_count,
                        row_tap : row_tap + row_count,
                        :,
                        col_tap : col_tap + columns,
                    ]
                    for col_tap in range(3)
                ],
                axis=2,
            )
            partials.append(
                jnp.einsum("thow,thkw->ok", out_grads, stacked, preferred_element_type=jnp.float32)
            )
    return jnp.stack(partials).reshape(3, 3, channels, 3, channels)


def spatial_transpose(kernel_slab, source):
    row_count = source.shape[1] - 2
    columns = source.shape[3] - 2
    channels = source.shape[2]
    summed = None
    for row_tap in range(3):
        stacked = jnp.concatenate(
            [
                source[
                    :, 2 - row_tap : 2 - row_tap + row_count, :, 2 - col_tap : 2 - col_tap + columns
                ]
                for col_tap in range(3)
            ],
            axis=2,
        )
        weights = kernel_slab[row_tap].transpose(1, 0, 2).reshape(3 * channels, channels)
        contrib = jnp.einsum("nhkw,ki->nhiw", stacked, weights, preferred_element_type=jnp.float32)
        summed = contrib if summed is None else summed + contrib
    return summed


def transpose_conv(kernel, source, number, offset):
    row_count = source.shape[1] - 2
    columns = source.shape[3] - 2
    channels = source.shape[2]
    summed = jnp.zeros((number, row_count, channels, columns), jnp.float32)
    for time_tap in range(3):
        first_out = max(0, time_tap - offset)
        last_out = min(number, source.shape[0] + time_tap - offset)
        window = source[first_out + offset - time_tap : last_out + offset - time_tap]
        summed = summed.at[first_out:last_out].add(spatial_transpose(kernel[time_tap], window))
    return summed


def send_following(out_grads):
    following = passed_along(out_grads[:2], "block", -1)
    return jnp.concatenate([out_grads, following], axis=0)


def shards(inputs, out_grads, kernel, norm_gain, norm_shift):
    frame_count, row_count, channels, columns = inputs.shape
    height = row_count * lax.axis_size("tile")
    number = height * columns * (channels // GROUPS)
    grouped = inputs.astype(jnp.float32).reshape(
        frame_count, row_count, GROUPS, channels // GROUPS, columns
    )
    sums, squares = lax.psum(
        (jnp.sum(grouped, axis=(1, 3, 4)), jnp.sum(grouped * grouped, axis=(1, 3, 4))), "tile"
    )
    center = sums / number
    spread = lax.rsqrt(squares / number - center * center + epsilon)
    normed, shaped = activate(inputs, center, spread, norm_gain, norm_shift)
    local_acts = jax.nn.silu(shaped).astype(jnp.bfloat16)
    cached = passed_along(local_acts[frame_count - 2 :], "block", 1)
    joined = jnp.concatenate([cached, local_acts], axis=0)
    joined = extended(joined, (("tile", 1),), 1)
    padded = jnp.pad(joined, ((0, 0), (0, 0), (0, 0), (1, 1)))
    weight_sum = kernel_terms(out_grads, padded)
    source = send_following(out_grads)
    grad_rims = extended(source, (("tile", 1),), 1)
    grad_pad = jnp.pad(grad_rims, ((0, 0), (0, 0), (0, 0), (1, 1)))
    act_grad = transpose_conv(kernel, grad_pad, frame_count, 2)
    logistic = jax.nn.sigmoid(shaped)
    pre_grad = act_grad * logistic * (1.0 + shaped * (1.0 - logistic))
    norm_grad = pre_grad * norm_gain[None, None, :, None]
    grouped_grad = norm_grad.reshape(frame_count, row_count, GROUPS, channels // GROUPS, columns)
    grouped_norm = normed.reshape(frame_count, row_count, GROUPS, channels // GROUPS, columns)
    first_sum, second_sum = lax.psum(
        (
            jnp.sum(grouped_grad, axis=(1, 3, 4)),
            jnp.sum(grouped_grad * grouped_norm, axis=(1, 3, 4)),
        ),
        "tile",
    )
    first_mean = (first_sum / number)[:, None, :, None, None]
    second_mean = (second_sum / number)[:, None, :, None, None]
    result = spread[:, None, :, None, None] * (
        grouped_grad - first_mean - grouped_norm * second_mean
    )
    input_grad = result.reshape(frame_count, row_count, channels, columns).astype(jnp.bfloat16)
    gain_local = jnp.sum(pre_grad * normed, axis=(0, 1, 3))
    shift_local = jnp.sum(pre_grad, axis=(0, 1, 3))
    kernel_sum, gain_sum, shift_sum = lax.psum(
        (weight_sum, gain_local, shift_local), ("block", "tile")
    )
    return (input_grad, kernel_sum / loss_scale, gain_sum / loss_scale, shift_sum / loss_scale)


def solution(mesh):
    placed = (P("block", "tile", None, None), P("block", "tile", None, None), P(), P(), P())
    return jax.shard_map(
        shards,
        mesh=mesh,
        in_specs=placed,
        out_specs=(P("block", "tile", None, None), P(), P(), P()),
        check_vma=False,
    )
```

profile of v0, /device:TPU:1, one launch (start us, length us, event | category | flops | bytes accessed | tf_op | source)
XLA Modules:
  0.0 469.5 jit_solution(9937415074539567423)
XLA Ops:
  7.2 1.0 slice.362
  8.2 1.3 collective-permute-start
  9.5 1.2 fusion.131
  11.2 69.1 %all-reduce.4 = (f32[4,32]{1,0:T(4,128)S(1)}, f32[4,32]{1,0:T(4,128)S(1)}) all-reduce(f32[4,32]{1,0:T(4,128)S(1)} %reduce_sum.73, f32[4,32]{1,0:T(4,128)S(1)} %reduce_sum.67), channel_id=1, replica_groups=mesh['block'=8,'tile'=32] {'tile'}, use_global_device_ids=true, to_apply=%region_5.6 | all-reduce | flops 256 | bytes 2048 | tf_op jit(solution)/shard_map/psum | solution.py:113
  80.4 7.2 %collective-permute-start.2 = (bf16[6,1,96,256]{3,2,1,0:T(8,128)(2,1)S(1)}, bf16[6,1,96,256]{3,2,1,0:T(8,128)(2,1)S(1)}, u32[]{:S(2)}, u32[]{:S(2)}) collective-permute-start(bf16[6,1,96,256]{3,2,1,0:T(8,128)(2,1)S(1)} %get-tuple-element.140), channel_id=1, source_target_pairs={{1,0},{2,1},{3,2},{4,3},{5,4},{6,5},{7,6},{8,7},{9,8},{10,9},{11,1... | collective-permute-start | bytes 884744 | tf_op jit(solution)/shard_map/ppermute | solution.py:27
  87.6 1.9 collective-permute-start.1
  90.0 3.2 collective-permute-done.1
  93.2 1.1 select_maximum_fusion.3
  94.2 1.6 fusion.177
  100.2 1.0 fusion.150
  101.6 62.9 %all-reduce.3 = (f32[4,32]{1,0:T(4,128)S(1)}, f32[4,32]{1,0:T(4,128)S(1)}) all-reduce(f32[4,32]{1,0:T(4,128)S(1)} %reduce_sum.93, f32[4,32]{1,0:T(4,128)S(1)} %reduce_sum.90), channel_id=1, replica_groups=mesh['block'=8,'tile'=32] {'tile'}, use_global_device_ids=true, to_apply=%region_11.12 | all-reduce | flops 256 | bytes 2048 | tf_op jit(solution)/shard_map/psum | solution.py:134
  164.9 1.2 fusion.145
  166.2 4.0 collective-permute-start.3
  170.2 2.6 collective-permute-done.3
  172.8 5.4 %collective-permute-start.5 = (bf16[6,1,96,256]{3,2,1,0:T(8,128)(2,1)S(1)}, bf16[6,1,96,256]{3,2,1,0:T(8,128)(2,1)S(1)}, u32[]{:S(2)}, u32[]{:S(2)}) collective-permute-start(bf16[6,1,96,256]{3,2,1,0:T(8,128)(2,1)S(1)} %get-tuple-element.134), channel_id=1, source_target_pairs={{1,0},{2,1},{3,2},{4,3},{5,4},{6,5},{7,6},{8,7},{9,8},{10,9},{11,1... | collective-permute-start | bytes 884744 | tf_op jit(solution)/shard_map/ppermute | solution.py:27
  178.2 2.1 collective-permute-start.4
  180.4 2.0 collective-permute-done.5
  182.4 1.4 collective-permute-done.4
  183.8 1.5 select_maximum_fusion
  185.3 1.6 fusion.176
  191.7 1.5 copy.64
  193.2 86.8 %all-reduce.2 = (f32[96]{0:T(128)S(1)}, f32[96]{0:T(128)S(1)}) all-reduce(f32[96]{0:T(128)S(1)} %get-tuple-element.64, f32[96]{0:T(128)S(1)} %get-tuple-element.67), channel_id=1, replica_groups=mesh['block'=8,'tile'=32] {'block','tile'}, use_global_device_ids=true, to_apply=%region_14.15 | all-reduce | flops 192 | bytes 1536 | tf_op jit(solution)/shard_map/psum | solution.py:149
  280.5 179.7 %all-reduce.7.cloned.1.call-done = f32[3,3,96,3,96]{4,2,3,1,0:T(8,128)} async-done(((f32[3,3,96,3,96]{4,2,3,1,0:T(8,128)}), f32[3,3,96,3,96]{4,2,3,1,0:T(8,128)}) %all-reduce.7.cloned.1.call-update) | async-done | bytes 995344 | tf_op jit(solution)/shard_map/psum | solution.py:149
  460.2 2.5 broadcast_multiply_fusion
  (62 shorter events, 11.4 us)
Async XLA Ops:
  7.2 73.1 %copy-start.1 = (bf16[4,2,96,256]{3,2,1,0:T(8,128)(2,1)S(1)}, bf16[4,2,96,256]{3,2,1,0:T(8,128)(2,1)}, u32[]{:S(2)}) copy-start(bf16[4,2,96,256]{3,2,1,0:T(8,128)(2,1)} %param.18) | copy-start | bytes 1179652
  7.2 453.0 %all-reduce.7.cloned.1.call-start = ((), (), s32[]{:S(2)}) async-start(), calls=%async_computation | async-start | bytes 2654208 | tf_op jit(solution)/shard_map/psum | solution.py:149
  8.2 72.1 %collective-permute-start = (bf16[2,2,96,256]{3,2,1,0:T(8,128)(2,1)S(1)}, bf16[2,2,96,256]{3,2,1,0:T(8,128)(2,1)S(1)}, u32[]{:S(2)}, u32[]{:S(2)}) collective-permute-start(bf16[2,2,96,256]{3,2,1,0:T(8,128)(2,1)S(1)} %slice.362), channel_id=1, source_target_pairs={{32,0},{64,32},{96,64},{128,96},{160,128},{192,160},{224,192},{33,... | collective-permute-start | bytes 589832 | tf_op jit(solution)/shard_map/ppermute | solution.py:16
  11.2 78.8 %copy-start.2 = (bf16[3,3,96,3,96]{4,2,3,1,0:T(8,128)(2,1)S(1)}, bf16[3,3,96,3,96]{4,2,3,1,0:T(8,128)(2,1)}, u32[]{:S(2)}) copy-start(bf16[3,3,96,3,96]{4,2,3,1,0:T(8,128)(2,1)} %param.19) | copy-start | bytes 1492996
  80.4 9.6 %collective-permute-start.2 = (bf16[6,1,96,256]{3,2,1,0:T(8,128)(2,1)S(1)}, bf16[6,1,96,256]{3,2,1,0:T(8,128)(2,1)S(1)}, u32[]{:S(2)}, u32[]{:S(2)}) collective-permute-start(bf16[6,1,96,256]{3,2,1,0:T(8,128)(2,1)S(1)} %get-tuple-element.140), channel_id=1, source_target_pairs={{1,0},{2,1},{3,2},{4,3},{5,4},{6,5},{7,6},{8,7},{9,8},{10,9},{11,1... | collective-permute-start | bytes 884744 | tf_op jit(solution)/shard_map/ppermute | solution.py:27
  87.6 5.6 %collective-permute-start.1 = (bf16[6,1,96,256]{3,2,1,0:T(8,128)(2,1)S(1)}, bf16[6,1,96,256]{3,2,1,0:T(8,128)(2,1)S(1)}, u32[]{:S(2)}, u32[]{:S(2)}) collective-permute-start(bf16[6,1,96,256]{3,2,1,0:T(8,128)(2,1)S(1)} %get-tuple-element.139), channel_id=1, source_target_pairs={{0,1},{1,2},{2,3},{3,4},{4,5},{5,6},{6,7},{7,8},{8,9},{9,10},{10,1... | collective-permute-start | bytes 884744 | tf_op jit(solution)/shard_map/ppermute | solution.py:24
  99.2 1.0 copy-start
  99.2 1.0 copy-start.3
  99.2 1.0 copy-start.4
  166.2 6.6 %collective-permute-start.3 = (bf16[2,2,96,256]{3,2,1,0:T(8,128)(2,1)S(1)}, bf16[2,2,96,256]{3,2,1,0:T(8,128)(2,1)S(1)}, u32[]{:S(2)}, u32[]{:S(2)}) collective-permute-start(bf16[2,2,96,256]{3,2,1,0:T(8,128)(2,1)S(1)} %slice.459), channel_id=1, source_target_pairs={{0,32},{32,64},{64,96},{96,128},{128,160},{160,192},{192,224},{1,3... | collective-permute-start | bytes 589832 | tf_op jit(solution)/shard_map/ppermute | solution.py:16
  172.8 9.5 %collective-permute-start.5 = (bf16[6,1,96,256]{3,2,1,0:T(8,128)(2,1)S(1)}, bf16[6,1,96,256]{3,2,1,0:T(8,128)(2,1)S(1)}, u32[]{:S(2)}, u32[]{:S(2)}) collective-permute-start(bf16[6,1,96,256]{3,2,1,0:T(8,128)(2,1)S(1)} %get-tuple-element.134), channel_id=1, source_target_pairs={{1,0},{2,1},{3,2},{4,3},{5,4},{6,5},{7,6},{8,7},{9,8},{10,9},{11,1... | collective-permute-start | bytes 884744 | tf_op jit(solution)/shard_map/ppermute | solution.py:27
  178.2 5.6 %collective-permute-start.4 = (bf16[6,1,96,256]{3,2,1,0:T(8,128)(2,1)S(1)}, bf16[6,1,96,256]{3,2,1,0:T(8,128)(2,1)S(1)}, u32[]{:S(2)}, u32[]{:S(2)}) collective-permute-start(bf16[6,1,96,256]{3,2,1,0:T(8,128)(2,1)S(1)} %get-tuple-element.133), channel_id=1, source_target_pairs={{0,1},{1,2},{2,3},{3,4},{4,5},{5,6},{6,7},{7,8},{8,9},{9,10},{10,1... | collective-permute-start | bytes 884744 | tf_op jit(solution)/shard_map/ppermute | solution.py:24
Sparse Core Ops, SparseCore 0:
  193.3 266.7 all-reduce.6
where the time goes:
time: 470 us
  blocking collectives  219 us (47%)
  waiting for transfers between devices  189 us (40%)
  starting transfers between devices  22 us (5%)
  between operations  14.5 us (3%)
  other arithmetic  8.95 us (2%)
  matrix products  8.78 us (2%)
  local copies, waits for them, and re-layouts  7.72 us (2%)
    psum x1, waiting for transfers between devices, shards(): lax.psum((weight_sum, gain_local, shift_local), ('block', 'tile'))  180 us
    psum x1, blocking collectives, shards(): lax.psum((weight_sum, gain_local, shift_local), ('block', 'tile'))  86.8 us
    psum x1, blocking collectives, shards(): lax.psum((jnp.sum(grouped, axis=(1, 3, 4)), jnp.sum(grouped * grouped, ax...  69.1 us
    psum x1, blocking collectives, shards(): lax.psum((jnp.sum(grouped_grad, axis=(1, 3, 4)), jnp.sum(grouped_grad * g...  62.9 us
    ppermute x2, starting transfers between devices, extended(): lax.ppermute(lax.slice_in_dim(block, 0, width, axis=dim), axis, backward)  12.6 us
  transfers between devices with their start and end apart: 7, of which 5 were waited for; matrix products, arithmetic and copies ran while one was open for 1% of the time, Pallas kernels for 0%

commit v1 on v0

v1 whole, which is shorter than its diff:
```python
import functools

import jax
import jax.numpy as jnp
from jax import lax
from jax.experimental import pallas as pl
from jax.experimental.pallas import tpu as pltpu
from jax.sharding import PartitionSpec as P

MESH = pl.DeviceIdType.MESH
GROUPS = 32
LOSS_SCALE = 1024.0
EPSILON = 1e-06
F32 = jnp.float32
BF16 = jnp.bfloat16

FRAMES, ROWS, CH, COLS = 4, 2, 96, 256
TAPS = 9 * CH
KEPT = TAPS // 4
SPLIT = TAPS - KEPT
FLAT = 2048
HALF = FLAT // 2


def group_sum(values, lane):
    place = lax.rem(lane, 3)
    one_up = pltpu.roll(values, 127, 1)
    two_up = pltpu.roll(values, 126, 1)
    one_down = pltpu.roll(values, 1, 1)
    two_down = pltpu.roll(values, 2, 1)
    first = jnp.where(place == 0, one_up, one_down)
    second = jnp.where(place == 2, two_down, jnp.where(place == 0, two_up, one_up))
    return values + first + second


def body(
    sizes,
    x_hbm, g_hbm, w_hbm, gain_ref, shift_ref,
    out_hbm, kg_hbm, small_ref,
    xv, gp, wv, wst, factor, normed, acts, acc, pre, outv,
    packed, core_send, core_got, plane_send, plane_got, z_send, z_got, fin_send, fin_got,
    final, plane_fin, kg_out, tmat, st_send, quad_got, st_mid, col_got, blk_send, blk_got,
    loc_sem, ssem, rsem,
):
    nb, nz = sizes
    ny = nb // 2
    plane = 2 * nb
    share = HALF // plane
    zshare = share // nz
    b = lax.axis_index("block")
    t = lax.axis_index("tile")
    nt = 4 * nz
    z = t // 4
    xh = lax.rem(t, 4) // 2
    c = lax.rem(t, 2)
    xl, y = b // ny, lax.rem(b, ny)
    flip_c = t + 1 - 2 * c
    flip_x = t + 2 - 4 * xh
    flip_cx = flip_c + 2 - 4 * xh
    across = lax.rem(t + nt - 1 + 2 * c, nt)
    b_up = lax.rem(b + 1, nb)
    b_down = lax.rem(b + nb - 1, nb)
    me = xh * nb + b

    counter = [0]

    def remote(src, dst, device):
        i = counter[0]
        counter[0] += 1
        return pltpu.make_async_remote_copy(
            src_ref=src, dst_ref=dst, send_sem=ssem.at[i], recv_sem=rsem.at[i],
            device_id=device, device_id_type=MESH,
        )

    def plane_at(dx, dy):
        x = lax.rem(2 * xh + xl + dx, 4)
        yy = lax.rem(y + dy, ny)
        hi, lo = x // 2, lax.rem(x, 2)
        block = lo * ny + yy
        return hi * nb + block, (block, t + 2 * (hi - xh))

    steps = [(dx, dy) for dx in range(4) for dy in range(ny) if (dx, dy) != (0, 0)]
    to_plane = [plane_at(dx, dy) for dx, dy in steps]
    from_plane = [plane_at((4 - dx) % 4, (ny - dy) % ny) for dx, dy in steps]

    load_x = pltpu.make_async_copy(x_hbm, xv, loc_sem.at[0])
    load_g = pltpu.make_async_copy(g_hbm, gp.at[pl.ds(0, FRAMES), pl.ds(1, ROWS)], loc_sem.at[1])
    load_w = pltpu.make_async_copy(w_hbm, wv, loc_sem.at[2])
    load_x.start()
    load_g.start()
    load_w.start()

    barrier = pltpu.get_barrier_semaphore()
    friends = [device for _, device in to_plane]
    for d in range(1, nz):
        friends.append((b, lax.rem(t + 4 * d, nt)))
    for tile in (flip_c, across):
        for block in (b, b_up, b_down):
            friends.append((block, tile))
    friends.append((b, flip_cx))
    for device in friends:
        pl.semaphore_signal(barrier, inc=1, device_id=device, device_id_type=MESH)

    lane = lax.broadcasted_iota(jnp.int32, (CH, 128), 1)
    lane8 = lax.broadcasted_iota(jnp.int32, (8, 128), 1)
    row8 = lax.broadcasted_iota(jnp.int32, (8, 128), 0)
    col = lax.broadcasted_iota(jnp.int32, (CH, COLS), 1)
    tmat[...] = jnp.zeros((128, 128), F32)

    def channel_tile(columns):
        table = jnp.zeros((CH, 128), F32)
        for k, value in enumerate(columns):
            table = jnp.where(lane == k, value, table)
        tmat[0:CH, :] = table
        return tmat[...].T[0:8, :]

    def channel_columns(tile):
        tmat[0:8, :] = tile
        return tmat[...].T[0:CH, :]

    def halved(value):
        return value[:, 0:128] + value[:, 128:256]

    load_x.wait()
    firsts, seconds = [], []
    for f in range(FRAMES):
        one, two = jnp.zeros((CH, 128), F32), jnp.zeros((CH, 128), F32)
        for r in range(ROWS):
            value = xv[f, r].astype(F32)
            one = one + halved(value)
            two = two + halved(value * value)
        firsts.append(jnp.sum(one, axis=1, keepdims=True))
        seconds.append(jnp.sum(two, axis=1, keepdims=True))
    st_send[0] = channel_tile(firsts + seconds)

    pl.semaphore_wait(barrier, len(friends))

    inner_low, inner_high = t > 0, t < nt - 1
    has_down, has_up = b > 0, b < nb - 1
    t_low, t_high = lax.rem(t + nt - 1, nt), lax.rem(t + 1, nt)
    four, two = pl.ds(0, FRAMES), pl.ds(0, 2)
    late = pl.ds(FRAMES, 2)
    halos = []
    for src, dst, device, sends, gets in (
        (g_hbm.at[four, 1], gp.at[four, 0], (b, t_high), inner_high, inner_low),
        (g_hbm.at[four, 0], gp.at[four, 3], (b, t_low), inner_low, inner_high),
        (g_hbm.at[two], gp.at[late, pl.ds(1, ROWS)], (b_down, t), has_down, has_up),
        (g_hbm.at[two, 1], gp.at[late, 0], (b_down, t_high),
         jnp.logical_and(has_down, inner_high), jnp.logical_and(has_up, inner_low)),
        (g_hbm.at[two, 0], gp.at[late, 3], (b_down, t_low),
         jnp.logical_and(has_down, inner_low), jnp.logical_and(has_up, inner_high)),
    ):
        halos.append((remote(src, dst, device), sends, gets))

    def all_sum(tile, at):
        quad = 2 * xh + c
        copies = []
        for k, other in enumerate((flip_c, flip_x, flip_cx)):
            slot = lax.rem(other, 4)
            copies.append((
                remote(st_send.at[at], quad_got.at[at, quad], (b, other)),
                quad_got.at[at, slot],
            ))
        for copy, _ in copies:
            copy.start()
        quad_got[at, quad] = tile
        return copies

    def quad_sum(copies, at):
        for copy, _ in copies:
            copy.wait_recv()
        total = quad_got[at, 0]
        for k in range(1, 4):
            total = total + quad_got[at, k]
        st_mid[at] = total
        out = []
        for d in range(1, nz):
            out.append(remote(st_mid.at[at], col_got.at[at, z], (b, lax.rem(t + 4 * d, nt))))
        for copy in out:
            copy.start()
        col_got[at, z] = total
        return out

    def col_sum(copies, at):
        for copy in copies:
            copy.wait_recv()
        total = col_got[at, 0]
        for k in range(1, nz):
            total = total + col_got[at, k]
        return total

    waiting = []
    stat_copies = all_sum(st_send[0], 0)
    for copy, sends, _ in halos:
        pl.when(sends)(copy.start)

    @pl.when(jnp.logical_not(inner_low))
    def _():
        gp[:, 0] = jnp.zeros((FRAMES + 2, CH, COLS), BF16)

    @pl.when(jnp.logical_not(inner_high))
    def _():
        gp[:, 3] = jnp.zeros((FRAMES + 2, CH, COLS), BF16)

    @pl.when(jnp.logical_not(has_up))
    def _():
        gp[late] = jnp.zeros((2, 4, CH, COLS), BF16)

    stat_copies_z = quad_sum(stat_copies, 0)
    waiting += [copy for copy, _ in stat_copies] + stat_copies_z

    load_w.wait()
    for r in range(3):
        slab = jnp.concatenate(
            [wv[2 - p, 2 - q, r] for p in range(3) for q in range(3)], axis=0
        )
        wst[r * CH : (r + 1) * CH, :] = slab.astype(F32).T.astype(BF16)

    number = float(nt * ROWS * COLS * (CH // GROUPS))
    sums = group_sum(col_sum(stat_copies_z, 0), lane8) / number
    center_rows = sums
    square_rows = pltpu.roll(sums, 4, 0)
    spread_rows = lax.rsqrt(square_rows - center_rows * center_rows + EPSILON)
    both = jnp.where(row8 < 4, center_rows, pltpu.roll(spread_rows, 4, 0))
    stats = channel_columns(both)
    vectors = jnp.where(
        row8 == 0,
        jnp.broadcast_to(gain_ref[...], (8, 128)),
        jnp.broadcast_to(shift_ref[...], (8, 128)),
    )
    vectors = channel_columns(vectors)
    gain, shift = vectors[:, 0:1], vectors[:, 1:2]

    acts[...] = jnp.zeros_like(acts)
    for f in range(FRAMES):
        center, spread = stats[:, f : f + 1], stats[:, 4 + f : 5 + f]
        for r in range(ROWS):
            n = f * ROWS + r
            scaled = (xv[f, r].astype(F32) - center) * spread
            shaped = scaled * gain + shift
            logistic = 1.0 / (1.0 + jnp.exp(-shaped))
            active = shaped * logistic
            normed[n] = scaled
            factor[n] = logistic * (1.0 + shaped * (1.0 - logistic))
            before = jnp.where(col == 0, 0.0, pltpu.roll(active, 1, 1))
            after = jnp.where(col == COLS - 1, 0.0, pltpu.roll(active, COLS - 1, 1))
            acts[n, 0:CH] = before.astype(BF16)
            acts[n, 128 : 128 + CH] = active.astype(BF16)
            acts[n, 256 : 256 + CH] = after.astype(BF16)

    load_g.wait()
    for copy, _, gets in halos:
        pl.when(gets)(copy.wait_recv)

    def kernel_term(n):
        f, r = n // ROWS, lax.rem(n, ROWS)
        window = gp[pl.ds(f, 3), pl.ds(r, 3)].reshape(TAPS, COLS)
        return lax.dot_general(
            window, acts[n], (((1,), (1,)), ((), ())), preferred_element_type=F32
        )

    acc[...] = kernel_term(0)

    @pl.loop(1, FRAMES * ROWS)
    def _(n):
        acc[...] += kernel_term(n)

    lanes = lax.broadcasted_iota(jnp.int32, (KEPT, 128), 1)
    for k in range(3):
        for s in range(3):
            row = KEPT * (3 * k + s)
            slab, first = row // TAPS, row % TAPS
            extra = acc[KEPT * (s + 1) : KEPT * (s + 2), 256:384]
            extra = pltpu.roll(extra, CH - 32 * k, 1)
            packed[row : row + KEPT] = jnp.where(
                lanes < CH, acc[first : first + KEPT, 128 * slab : 128 * slab + 128], extra
            )
    packed[9 * KEPT : FLAT] = jnp.zeros((FLAT - 9 * KEPT, 128), F32)

    mine = pl.multiple_of(c * HALF, HALF)
    theirs = pl.multiple_of((1 - c) * HALF, HALF)
    core_send[...] = packed[pl.ds(theirs, HALF)].astype(BF16)
    core_copy = remote(core_send, core_got, (b, flip_c))
    core_copy.start()

    @pl.loop(0, FRAMES * ROWS)
    def _(n):
        f, r = n // ROWS, lax.rem(n, ROWS)
        window = gp[pl.ds(f, 3), pl.ds(r, 3)].reshape(TAPS, COLS)
        product = jnp.dot(wst[...], window, preferred_element_type=F32)
        after = pltpu.roll(product[0:CH], COLS - 1, 1)
        before = pltpu.roll(product[2 * CH : 3 * CH], 1, 1)
        after = jnp.where(col == COLS - 1, 0.0, after)
        before = jnp.where(col == 0, 0.0, before)
        pre[n] = (after + product[CH : 2 * CH] + before) * factor[n]

    core_copy.wait_recv()
    chip = packed[pl.ds(mine, HALF)] + core_got[...].astype(F32)
    packed[pl.ds(mine, HALF)] = chip
    plane_send[...] = chip.astype(BF16)
    plane_copies = []
    for k, (place, device) in enumerate(to_plane):
        rows = pl.ds(pl.multiple_of(place * share, share), share)
        plane_copies.append(remote(plane_send.at[rows], plane_got.at[k], device))
    for copy in plane_copies:
        copy.start()

    firsts, seconds = [], []
    for f in range(FRAMES):
        one, two = jnp.zeros((CH, 128), F32), jnp.zeros((CH, 128), F32)
        for r in range(ROWS):
            n = f * ROWS + r
            value = pre[n]
            one = one + halved(value)
            two = two + halved(value * normed[n])
        firsts.append(jnp.sum(one, axis=1, keepdims=True))
        seconds.append(jnp.sum(two, axis=1, keepdims=True))
    tmat[...] = jnp.zeros((128, 128), F32)
    st_send[1] = channel_tile(firsts + seconds)
    stat_copies = all_sum(st_send[1], 1)

    for copy in plane_copies:
        copy.wait_recv()
    part = packed[pl.ds(pl.multiple_of(mine + me * share, share), share)]
    for k in range(plane - 1):
        part = part + plane_got[k].astype(F32)
    z_send[...] = part
    z_copies = []
    for d in range(1, nz):
        there = lax.rem(z + d, nz)
        rows = pl.ds(pl.multiple_of(there * zshare, zshare), zshare)
        z_copies.append(remote(z_send.at[rows], z_got.at[d], (b, lax.rem(t + 4 * d, nt))))
    for copy in z_copies:
        copy.start()

    stat_copies_z = quad_sum(stat_copies, 1)
    waiting += [copy for copy, _ in stat_copies] + stat_copies_z

    for copy in z_copies:
        copy.wait_recv()
    here = pl.ds(pl.multiple_of(z * zshare, zshare), zshare)
    part = z_send[here]
    for d in range(1, nz):
        part = part + z_got[d]
    fin_send[...] = part
    fin_got[here] = part
    fin_copies = []
    for d in range(1, nz):
        fin_copies.append(remote(fin_send, fin_got.at[here], (b, lax.rem(t + 4 * d, nt))))
    for copy in fin_copies:
        copy.start()

    total = col_sum(stat_copies_z, 1)
    gain_rows = jnp.broadcast_to(gain_ref[...], (8, 128))
    means = channel_columns(group_sum(total * gain_rows, lane8) / number)

    pairs = total + pltpu.roll(total, 2, 0)
    pairs = pairs + pltpu.roll(pairs, 1, 0)
    blk_send[...] = pairs
    blk_got[b] = pairs
    blk_copies = []
    for d in range(1, nb):
        block = lax.rem(b + d, nb)
        blk_copies.append(remote(blk_send, blk_got.at[b], (block, t)))
    for copy in blk_copies:
        copy.start()

    for copy in fin_copies:
        copy.wait_recv()
    plane_fin[...] = fin_got[...].astype(BF16)
    own_rows = pl.ds(pl.multiple_of(mine + me * share, share), share)
    final[own_rows] = plane_fin[...]
    spread_copies = []
    for place, device in to_plane:
        spread_copies.append(remote(plane_fin, final.at[own_rows], device))
    for copy in spread_copies:
        copy.start()
    pass_copies = [remote(plane_fin, final.at[own_rows], (b, flip_c))]
    pass_copies[0].start()

    for f in range(FRAMES):
        spread = stats[:, 4 + f : 5 + f]
        m1, m2 = means[:, f : f + 1], means[:, 4 + f : 5 + f]
        for r in range(ROWS):
            n = f * ROWS + r
            value = spread * (pre[n] * gain - m1 - normed[n] * m2)
            outv[f, r] = value.astype(BF16)
    store_x = pltpu.make_async_copy(outv, out_hbm, loc_sem.at[3])
    store_x.start()

    for copy in blk_copies:
        copy.wait_recv()
    total = blk_got[0]
    for k in range(1, nb):
        total = total + blk_got[k]
    small_ref[...] = total / LOSS_SCALE

    for copy, (place, _) in zip(spread_copies, from_plane):
        copy.wait_recv()
        rows = pl.ds(pl.multiple_of(mine + place * share, share), share)
        pass_copies.append(remote(final.at[rows], final.at[rows], (b, flip_c)))
        pass_copies[-1].start()
    for copy in pass_copies:
        copy.wait_recv()

    packed[...] = final[...].astype(F32) * (1.0 / LOSS_SCALE)
    for p in range(3):
        for q in range(3):
            tap = (2 - p) * 3 + (2 - q)
            for r in range(2):
                row = r * TAPS + tap * CH
                kg_out[p, q, r] = packed[row : row + CH, 0:CH]
    for tap in range(9):
        p, q = 2 - tap // 3, 2 - tap % 3
        for first in range(tap * CH, tap * CH + CH, 8):
            local = first - tap * CH
            if first < KEPT:
                slab = packed[2 * TAPS + first : 2 * TAPS + first + 8]
            else:
                slab = jnp.zeros((8, 128), F32)
                for k in range(3):
                    row = 3 * KEPT * k + first - KEPT
                    piece = pltpu.roll(packed[row : row + 8], 32 + 32 * k, 1)
                    slab = jnp.where(lane8 // 32 == k, piece, slab)
            kg_out[p, q, 2, local : local + 8] = slab[:, 0:CH]
    store_k = pltpu.make_async_copy(kg_out, kg_hbm, loc_sem.at[4])
    store_k.start()

    for copy, sends, _ in halos:
        pl.when(sends)(copy.wait_send)
    waiting += [core_copy] + plane_copies + z_copies + fin_copies + blk_copies
    waiting += spread_copies + pass_copies
    for copy in waiting:
        copy.wait_send()
    store_x.wait()
    store_k.wait()


def shards(sizes, inputs, out_grads, kernel, norm_gain, norm_shift):
    nb, nz = sizes
    plane = 2 * nb
    share = HALF // plane
    copies = 5 + 2 * (3 + nz - 1) + 1 + 2 * (plane - 1) + 2 * (nz - 1) + nb - 1 + plane
    vmem = pltpu.VMEM
    pad = lambda v: jnp.pad(v, (0, 128 - CH)).reshape(1, 128)
    any_space = pl.BlockSpec(memory_space=pl.ANY)
    in_vmem = pl.BlockSpec(memory_space=pltpu.VMEM)
    cells = FRAMES * ROWS
    out, grad, small = pl.pallas_call(
        functools.partial(body, sizes),
        out_shape=(
            jax.ShapeDtypeStruct((FRAMES, ROWS, CH, COLS), BF16),
            jax.ShapeDtypeStruct((3, 3, 3, CH, CH), F32),
            jax.ShapeDtypeStruct((8, 128), F32),
        ),
        in_specs=[any_space] * 3 + [in_vmem] * 2,
        out_specs=(any_space, any_space, in_vmem),
        scratch_shapes=[
            vmem((FRAMES, ROWS, CH, COLS), BF16),
            vmem((FRAMES + 2, ROWS + 2, CH, COLS), BF16),
            vmem((3, 3, 3, CH, CH), BF16),
            vmem((3 * CH, TAPS), BF16),
            vmem((cells, CH, COLS), F32),
            vmem((cells, CH, COLS), F32),
            vmem((cells, 3 * 128, COLS), BF16),
            vmem((TAPS, 3 * 128), F32),
            vmem((cells, CH, COLS), F32),
            vmem((FRAMES, ROWS, CH, COLS), BF16),
            vmem((FLAT, 128), F32),
            vmem((HALF, 128), BF16),
            vmem((HALF, 128), BF16),
            vmem((HALF, 128), BF16),
            vmem((plane - 1, share, 128), BF16),
            vmem((share, 128), F32),
            vmem((nz, share // nz, 128), F32),
            vmem((share // nz, 128), F32),
            vmem((share, 128), F32),
            vmem((FLAT, 128), BF16),
            vmem((share, 128), BF16),
            vmem((3, 3, 3, CH, CH), F32),
            vmem((128, 128), F32),
            vmem((2, 8, 128), F32),
            vmem((2, 4, 8, 128), F32),
            vmem((2, 8, 128), F32),
            vmem((2, nz, 8, 128), F32),
            vmem((8, 128), F32),
            vmem((nb, 8, 128), F32),
            pltpu.SemaphoreType.DMA((5,)),
            pltpu.SemaphoreType.DMA((copies,)),
            pltpu.SemaphoreType.DMA((copies,)),
        ],
        compiler_params=pltpu.CompilerParams(
            collective_id=0, has_side_effects=True, vmem_limit_bytes=40 * 1024 * 1024
        ),
    )(inputs, out_grads, kernel.transpose(0, 1, 3, 2, 4), pad(norm_gain), pad(norm_shift))
    return (out, grad.transpose(0, 1, 3, 2, 4), small[7, :CH], small[3, :CH])


def solution(mesh):
    sizes = (mesh.shape["block"], mesh.shape["tile"] // 4)
    placed = (P("block", "tile", None, None), P("block", "tile", None, None), P(), P(), P())
    return jax.shard_map(
        functools.partial(shards, sizes),
        mesh=mesh,
        in_specs=placed,
        out_specs=(P("block", "tile", None, None), P(), P(), P()),
        check_vma=False,
    )
```

time: 470 us -> 62 us (0.13)
  blocking collectives: 219 us -> 0 us
  waiting for transfers between devices: 189 us -> 0 us
  Pallas kernels: 0 us -> 55.1 us
  starting transfers between devices: 22 us -> 0 us
  between operations: 14.5 us -> 0.64 us
  other arithmetic: 8.95 us -> 0 us
  matrix products: 8.78 us -> 0 us
    psum x3 -> x0, blocking collectives: 219 us -> none  [the longest x1 86.8 us: shards(): lax.psum((weight_sum, gain_local, shift_local), ('block', 'tile'))]
    psum x1 -> x0, waiting for transfers between devices: 180 us -> none  [shards(): lax.psum((weight_sum, gain_local, shift_local), ('block', 'tile'))]
    pallas_call x0 -> x1, Pallas kernels: none -> 55.1 us  [shards(): pl.pallas_call(functools.partial(body, sizes), out_shape=(jax.ShapeDtypeS...]
    ppermute x6 -> x0, starting transfers between devices: 21.9 us -> none  [the longest x2 12.6 us: extended(): lax.ppermute(lax.slice_in_dim(block, 0, width, axis=dim), axis, backward)]
    ppermute x6 -> x0, waiting for transfers between devices: 9.18 us -> none  [the longest x2 4.6 us: extended(): lax.ppermute(lax.slice_in_dim(block, block.shape[dim] - width, None, axis...]
    dot_general x18 -> x0, matrix products: 8.78 us -> none  [the longest x9 4.63 us: spatial_transpose(): jnp.einsum('nhkw,ki->nhiw', stacked, weights, preferred_element_type=jnp....]
  transfers between devices with their start and end apart: 7 -> 0, of which waited for: 5 -> 0; matrix products, arithmetic and copies ran while one was open for 1% -> 0% of each run, Pallas kernels for 0% -> 0%
where the time goes in v1:
time: 62 us; the launch traced here: 61.8 us
  Pallas kernels  55.1 us (89%)
  local copies, waits for them, and re-layouts  6.08 us (10%)
  between operations  0.64 us (1%)
    pallas_call x1, Pallas kernels, shards(): pl.pallas_call(functools.partial(body, sizes), out_shape=(jax.ShapeDtypeS...  55.1 us
    unnamed x8, local copies, waits for them, and re-layouts  4.89 us

profile of v1, /device:TPU:1, one launch (start us, length us, event | category | flops | bytes accessed | tf_op | source)
XLA Modules:
  0.0 61.8 jit_solution(12413917526038650964)
XLA Ops:
  0.6 0.7 %pad_bitcast_fusion = (f32[1,128]{1,0:T(1,128)S(1)}, f32[1,128]{1,0:T(1,128)S(1)}) fusion(f32[96]{0:T(128)} %param.9, f32[96]{0:T(128)} %param.8), kind=kLoop, calls=%fused_computation.2 | loop fusion | bytes 1792 | tf_op jit(solution)/shard_map/reshape | solution.py:445
  1.3 0.0 copy-start
  1.3 1.1 %copy-done = bf16[3,3,96,3,96]{4,2,3,1,0:T(8,128)(2,1)S(1)} copy-done((bf16[3,3,96,3,96]{4,2,3,1,0:T(8,128)(2,1)S(1)}, bf16[3,3,96,3,96]{4,2,3,1,0:T(8,128)(2,1)}, u32[]{:S(2)}) %copy-start) | copy-done | bytes 497688
  2.4 0.0 copy-start.1
  2.4 1.0 %copy-done.1 = bf16[4,2,96,256]{3,2,1,0:T(8,128)(2,1)S(1)} copy-done((bf16[4,2,96,256]{3,2,1,0:T(8,128)(2,1)S(1)}, bf16[4,2,96,256]{3,2,1,0:T(8,128)(2,1)}, u32[]{:S(2)}) %copy-start.1) | copy-done | bytes 393240
  3.4 0.0 copy-start.2
  3.4 1.0 %copy-done.2 = bf16[4,2,96,256]{3,2,1,0:T(8,128)(2,1)S(1)} copy-done((bf16[4,2,96,256]{3,2,1,0:T(8,128)(2,1)S(1)}, bf16[4,2,96,256]{3,2,1,0:T(8,128)(2,1)}, u32[]{:S(2)}) %copy-start.2) | copy-done | bytes 393240
  4.4 55.1 %shard_map.84 = (bf16[4,2,96,256]{3,2,1,0:T(8,128)(2,1)S(1)}, f32[3,3,3,96,96]{4,3,2,1,0:T(8,128)S(1)}, f32[8,128]{1,0:T(8,128)S(1)}) custom-call(bf16[4,2,96,256]{3,2,1,0:T(8,128)(2,1)S(1)} %copy-done.1, bf16[4,2,96,256]{3,2,1,0:T(8,128)(2,1)S(1)} %copy-done.2, bf16[3,3,3,96,96]{4,3,2,1,0:T(8,128)(2,1)S(1)} %bitcast.11, ...), custom_call_target="tpu_custom_call" | custom-call | tf_op jit(solution)/shard_map/pallas_call | solution.py:449
  59.5 0.5 slice_bitcast_fusion
  60.0 0.7 %copy.11 = bf16[4,2,96,256]{3,2,1,0:T(8,128)(2,1)} copy(bf16[4,2,96,256]{3,2,1,0:T(8,128)(2,1)S(1)} %get-tuple-element.18) | data formatting | bytes 786432
  60.7 1.1 %copy.12 = f32[3,3,96,3,96]{4,2,3,1,0:T(8,128)} copy(f32[3,3,96,3,96]{4,2,3,1,0:T(8,128)S(1)} %bitcast.10) | data formatting | bytes 1990656
Async XLA Ops:
  1.3 1.1 %copy-start = (bf16[3,3,96,3,96]{4,2,3,1,0:T(8,128)(2,1)S(1)}, bf16[3,3,96,3,96]{4,2,3,1,0:T(8,128)(2,1)}, u32[]{:S(2)}) copy-start(bf16[3,3,96,3,96]{4,2,3,1,0:T(8,128)(2,1)} %param.7) | copy-start | bytes 1492996
  2.4 1.0 %copy-start.1 = (bf16[4,2,96,256]{3,2,1,0:T(8,128)(2,1)S(1)}, bf16[4,2,96,256]{3,2,1,0:T(8,128)(2,1)}, u32[]{:S(2)}) copy-start(bf16[4,2,96,256]{3,2,1,0:T(8,128)(2,1)} %x_hbm.1) | copy-start | bytes 1179652
  3.4 1.0 %copy-start.2 = (bf16[4,2,96,256]{3,2,1,0:T(8,128)(2,1)S(1)}, bf16[4,2,96,256]{3,2,1,0:T(8,128)(2,1)}, u32[]{:S(2)}) copy-start(bf16[4,2,96,256]{3,2,1,0:T(8,128)(2,1)} %g_hbm.1) | copy-start | bytes 1179652

commit v2 on v1

--- a/solution.py
+++ b/solution.py
@@ -16,8 +16,9 @@
 
 FRAMES, ROWS, CH, COLS = 4, 2, 96, 256
 TAPS = 9 * CH
-KEPT = TAPS // 4
-SPLIT = TAPS - KEPT
+KEPT = 240
+MOVED = TAPS - KEPT
+SEG = 48
 FLAT = 2048
 HALF = FLAT // 2
 
@@ -35,18 +36,17 @@
 
 def body(
     sizes,
-    x_hbm, g_hbm, w_hbm, gain_ref, shift_ref,
-    out_hbm, kg_hbm, small_ref,
-    xv, gp, wv, wst, factor, normed, acts, acc, pre, outv,
-    packed, core_send, core_got, plane_send, plane_got, z_send, z_got, fin_send, fin_got,
-    final, plane_fin, kg_out, tmat, st_send, quad_got, st_mid, col_got, blk_send, blk_got,
+    x_hbm, g_hbm, w_hbm, gain_hbm, shift_hbm,
+    out_hbm, fin_hbm, small_hbm,
+    gain_ref, shift_ref, outv, small_ref, xv, gp, wv, wst, factor, normed, acts, acc, pre,
+    packed, core_send, core_got, plane_send, plane_got, z_send, z_got,
+    final, plane_fin, tmat, st_send, quad_got, st_mid, col_got, blk_send, blk_got,
     loc_sem, ssem, rsem,
 ):
     nb, nz = sizes
     ny = nb // 2
     plane = 2 * nb
     share = HALF // plane
-    zshare = share // nz
     b = lax.axis_index("block")
     t = lax.axis_index("tile")
     nt = 4 * nz
@@ -80,24 +80,27 @@
         return hi * nb + block, (block, t + 2 * (hi - xh))
 
     steps = [(dx, dy) for dx in range(4) for dy in range(ny) if (dx, dy) != (0, 0)]
+    steps.sort(key=lambda d: -min(d[0], 4 - d[0]) - min(d[1], ny - d[1]))
     to_plane = [plane_at(dx, dy) for dx, dy in steps]
     from_plane = [plane_at((4 - dx) % 4, (ny - dy) % ny) for dx, dy in steps]
 
     load_x = pltpu.make_async_copy(x_hbm, xv, loc_sem.at[0])
     load_g = pltpu.make_async_copy(g_hbm, gp.at[pl.ds(0, FRAMES), pl.ds(1, ROWS)], loc_sem.at[1])
     load_w = pltpu.make_async_copy(w_hbm, wv, loc_sem.at[2])
+    load_gain = pltpu.make_async_copy(gain_hbm, gain_ref, loc_sem.at[3])
+    load_shift = pltpu.make_async_copy(shift_hbm, shift_ref, loc_sem.at[4])
     load_x.start()
     load_g.start()
+    load_gain.start()
+    load_shift.start()
     load_w.start()
 
     barrier = pltpu.get_barrier_semaphore()
     friends = [device for _, device in to_plane]
-    for d in range(1, nz):
-        friends.append((b, lax.rem(t + 4 * d, nt)))
-    for tile in (flip_c, across):
-        for block in (b, b_up, b_down):
-            friends.append((block, tile))
-    friends.append((b, flip_cx))
+    far_first = sorted(range(1, nz), key=lambda d: -min(d, nz - d))
+    column = [(b, lax.rem(t + 4 * d, nt)) for d in far_first]
+    friends += column
+    friends += [(b, across), (b_up, across), (b_down, across), (b, flip_c), (b, flip_cx)]
     for device in friends:
         pl.semaphore_signal(barrier, inc=1, device_id=device, device_id_type=MESH)
 
@@ -135,22 +138,15 @@
 
     pl.semaphore_wait(barrier, len(friends))
 
-    inner_low, inner_high = t > 0, t < nt - 1
+    has_across = jnp.where(c == 0, t > 0, t < nt - 1)
     has_down, has_up = b > 0, b < nb - 1
-    t_low, t_high = lax.rem(t + nt - 1, nt), lax.rem(t + 1, nt)
-    four, two = pl.ds(0, FRAMES), pl.ds(0, 2)
-    late = pl.ds(FRAMES, 2)
-    halos = []
-    for src, dst, device, sends, gets in (
-        (g_hbm.at[four, 1], gp.at[four, 0], (b, t_high), inner_high, inner_low),
-        (g_hbm.at[four, 0], gp.at[four, 3], (b, t_low), inner_low, inner_high),
-        (g_hbm.at[two], gp.at[late, pl.ds(1, ROWS)], (b_down, t), has_down, has_up),
-        (g_hbm.at[two, 1], gp.at[late, 0], (b_down, t_high),
-         jnp.logical_and(has_down, inner_high), jnp.logical_and(has_up, inner_low)),
-        (g_hbm.at[two, 0], gp.at[late, 3], (b_down, t_low),
-         jnp.logical_and(has_down, inner_low), jnp.logical_and(has_up, inner_high)),
-    ):
-        halos.append((remote(src, dst, device), sends, gets))
+    four, two, late = pl.ds(0, FRAMES), pl.ds(0, 2), pl.ds(FRAMES, 2)
+    core_edge, far_edge = 3 - 3 * c, 3 * c
+    rows_far = remote(g_hbm.at[four, c], gp.at[four, 3 - 3 * c], (b, across))
+    rows_core = remote(g_hbm.at[four, 1 - c], gp.at[four, 3 * c], (b, flip_c))
+    next_two = remote(g_hbm.at[two], gp.at[late, pl.ds(1, ROWS)], (b_down, t))
+    corner_far = remote(g_hbm.at[two, c], gp.at[late, 3 - 3 * c], (b_down, across))
+    corner_core = remote(gp.at[late, 2 - c], gp.at[late, 3 * c], (b, flip_c))
 
     def all_sum(tile, at):
         quad = 2 * xh + c
@@ -174,8 +170,8 @@
             total = total + quad_got[at, k]
         st_mid[at] = total
         out = []
-        for d in range(1, nz):
-            out.append(remote(st_mid.at[at], col_got.at[at, z], (b, lax.rem(t + 4 * d, nt))))
+        for device in column:
+            out.append(remote(st_mid.at[at], col_got.at[at, z], device))
         for copy in out:
             copy.start()
         col_got[at, z] = total
@@ -191,21 +187,21 @@
 
     waiting = []
     stat_copies = all_sum(st_send[0], 0)
-    for copy, sends, _ in halos:
-        pl.when(sends)(copy.start)
-
-    @pl.when(jnp.logical_not(inner_low))
+    pl.when(has_down)(next_two.start)
+    pl.when(has_across)(rows_far.start)
+    rows_core.start()
+    pl.when(jnp.logical_and(has_down, has_across))(corner_far.start)
+
+    @pl.when(jnp.logical_not(has_across))
     def _():
-        gp[:, 0] = jnp.zeros((FRAMES + 2, CH, COLS), BF16)
-
-    @pl.when(jnp.logical_not(inner_high))
-    def _():
-        gp[:, 3] = jnp.zeros((FRAMES + 2, CH, COLS), BF16)
+        gp[:, far_edge] = jnp.zeros((FRAMES + 2, CH, COLS), BF16)
 
     @pl.when(jnp.logical_not(has_up))
     def _():
         gp[late] = jnp.zeros((2, 4, CH, COLS), BF16)
 
+    acc[...] = jnp.zeros_like(acc)
+    acts[...] = jnp.zeros_like(acts)
     stat_copies_z = quad_sum(stat_copies, 0)
     waiting += [copy for copy, _ in stat_copies] + stat_copies_z
 
@@ -222,16 +218,16 @@
     square_rows = pltpu.roll(sums, 4, 0)
     spread_rows = lax.rsqrt(square_rows - center_rows * center_rows + EPSILON)
     both = jnp.where(row8 < 4, center_rows, pltpu.roll(spread_rows, 4, 0))
+    tmat[...] = jnp.zeros((128, 128), F32)
     stats = channel_columns(both)
-    vectors = jnp.where(
-        row8 == 0,
-        jnp.broadcast_to(gain_ref[...], (8, 128)),
-        jnp.broadcast_to(shift_ref[...], (8, 128)),
-    )
-    vectors = channel_columns(vectors)
+    load_gain.wait()
+    load_shift.wait()
+    tmat[0:1, 0:CH] = gain_ref[...]
+    tmat[1:2, 0:CH] = shift_ref[...]
+    gain_rows = jnp.broadcast_to(tmat[0:1, :], (8, 128))
+    vectors = tmat[...].T[0:CH, :]
     gain, shift = vectors[:, 0:1], vectors[:, 1:2]
 
-    acts[...] = jnp.zeros_like(acts)
     for f in range(FRAMES):
         center, spread = stats[:, f : f + 1], stats[:, 4 + f : 5 + f]
         for r in range(ROWS):
@@ -248,34 +244,52 @@
             acts[n, 128 : 128 + CH] = active.astype(BF16)
             acts[n, 256 : 256 + CH] = after.astype(BF16)
 
+    def kernel_terms(late_frames, edge_rows):
+        for f in range(FRAMES):
+            lo, hi = (max(f, FRAMES), f + 3) if late_frames else (f, min(f + 3, FRAMES))
+            if lo >= hi:
+                continue
+            for r in range(ROWS):
+                if edge_rows:
+                    top, rows = 3 * r, 1
+                else:
+                    top, rows = 1, 2
+                window = gp[lo:hi, top : top + rows].reshape((hi - lo) * rows * CH, COLS)
+                product = lax.dot_general(
+                    window, acts[f * ROWS + r], (((1,), (1,)), ((), ())),
+                    preferred_element_type=F32,
+                )
+                height = rows * CH
+                for k in range(hi - lo):
+                    row = (3 * (lo + k - f) + top - r) * CH
+                    acc[row : row + height] += product[k * height : (k + 1) * height]
+
     load_g.wait()
-    for copy, _, gets in halos:
-        pl.when(gets)(copy.wait_recv)
-
-    def kernel_term(n):
-        f, r = n // ROWS, lax.rem(n, ROWS)
-        window = gp[pl.ds(f, 3), pl.ds(r, 3)].reshape(TAPS, COLS)
-        return lax.dot_general(
-            window, acts[n], (((1,), (1,)), ((), ())), preferred_element_type=F32
-        )
-
-    acc[...] = kernel_term(0)
-
-    @pl.loop(1, FRAMES * ROWS)
-    def _(n):
-        acc[...] += kernel_term(n)
-
-    lanes = lax.broadcasted_iota(jnp.int32, (KEPT, 128), 1)
-    for k in range(3):
-        for s in range(3):
-            row = KEPT * (3 * k + s)
-            slab, first = row // TAPS, row % TAPS
-            extra = acc[KEPT * (s + 1) : KEPT * (s + 2), 256:384]
-            extra = pltpu.roll(extra, CH - 32 * k, 1)
-            packed[row : row + KEPT] = jnp.where(
-                lanes < CH, acc[first : first + KEPT, 128 * slab : 128 * slab + 128], extra
-            )
-    packed[9 * KEPT : FLAT] = jnp.zeros((FLAT - 9 * KEPT, 128), F32)
+    kernel_terms(False, False)
+
+    @pl.when(has_up)
+    def _():
+        next_two.wait_recv()
+        corner_core.start()
+
+    kernel_terms(True, False)
+    rows_core.wait_recv()
+    pl.when(has_across)(rows_far.wait_recv)
+    kernel_terms(False, True)
+    pl.when(has_up)(corner_core.wait_recv)
+    pl.when(jnp.logical_and(has_up, has_across))(corner_far.wait_recv)
+    kernel_terms(True, True)
+
+    lanes = lax.broadcasted_iota(jnp.int32, (SEG, 128), 1)
+    for row in range(0, 2 * TAPS + KEPT, SEG):
+        slab, first = row // TAPS, row % TAPS
+        value = acc[first : first + SEG, 128 * slab : 128 * slab + 128]
+        k, source = row // MOVED, KEPT + row % MOVED
+        if k < 3:
+            extra = pltpu.roll(acc[source : source + SEG, 256:384], CH - 32 * k, 1)
+            value = jnp.where(lanes < CH, value, extra)
+        packed[row : row + SEG] = value
+    packed[2 * TAPS + KEPT : FLAT] = jnp.zeros((FLAT - 2 * TAPS - KEPT, 128), F32)
 
     mine = pl.multiple_of(c * HALF, HALF)
     theirs = pl.multiple_of((1 - c) * HALF, HALF)
@@ -324,34 +338,16 @@
     part = packed[pl.ds(pl.multiple_of(mine + me * share, share), share)]
     for k in range(plane - 1):
         part = part + plane_got[k].astype(F32)
-    z_send[...] = part
-    z_copies = []
-    for d in range(1, nz):
-        there = lax.rem(z + d, nz)
-        rows = pl.ds(pl.multiple_of(there * zshare, zshare), zshare)
-        z_copies.append(remote(z_send.at[rows], z_got.at[d], (b, lax.rem(t + 4 * d, nt))))
+    z_send[...] = part.astype(BF16)
+    z_got[z] = part.astype(BF16)
+    z_copies = [remote(z_send, z_got.at[z], device) for device in column]
     for copy in z_copies:
         copy.start()
 
     stat_copies_z = quad_sum(stat_copies, 1)
     waiting += [copy for copy, _ in stat_copies] + stat_copies_z
 
-    for copy in z_copies:
-        copy.wait_recv()
-    here = pl.ds(pl.multiple_of(z * zshare, zshare), zshare)
-    part = z_send[here]
-    for d in range(1, nz):
-        part = part + z_got[d]
-    fin_send[...] = part
-    fin_got[here] = part
-    fin_copies = []
-    for d in range(1, nz):
-        fin_copies.append(remote(fin_send, fin_got.at[here], (b, lax.rem(t + 4 * d, nt))))
-    for copy in fin_copies:
-        copy.start()
-
     total = col_sum(stat_copies_z, 1)
-    gain_rows = jnp.broadcast_to(gain_ref[...], (8, 128))
     means = channel_columns(group_sum(total * gain_rows, lane8) / number)
 
     pairs = total + pltpu.roll(total, 2, 0)
@@ -365,9 +361,12 @@
     for copy in blk_copies:
         copy.start()
 
-    for copy in fin_copies:
+    for copy in z_copies:
         copy.wait_recv()
-    plane_fin[...] = fin_got[...].astype(BF16)
+    part = z_got[0].astype(F32)
+    for k in range(1, nz):
+        part = part + z_got[k].astype(F32)
+    plane_fin[...] = (part * (1.0 / LOSS_SCALE)).astype(BF16)
     own_rows = pl.ds(pl.multiple_of(mine + me * share, share), share)
     final[own_rows] = plane_fin[...]
     spread_copies = []
@@ -385,7 +384,7 @@
             n = f * ROWS + r
             value = spread * (pre[n] * gain - m1 - normed[n] * m2)
             outv[f, r] = value.astype(BF16)
-    store_x = pltpu.make_async_copy(outv, out_hbm, loc_sem.at[3])
+    store_x = pltpu.make_async_copy(outv, out_hbm, loc_sem.at[5])
     store_x.start()
 
     for copy in blk_copies:
@@ -394,6 +393,8 @@
     for k in range(1, nb):
         total = total + blk_got[k]
     small_ref[...] = total / LOSS_SCALE
+    store_small = pltpu.make_async_copy(small_ref, small_hbm, loc_sem.at[6])
+    store_small.start()
 
     for copy, (place, _) in zip(spread_copies, from_plane):
         copy.wait_recv()
@@ -403,59 +404,81 @@
     for copy in pass_copies:
         copy.wait_recv()
 
-    packed[...] = final[...].astype(F32) * (1.0 / LOSS_SCALE)
-    for p in range(3):
-        for q in range(3):
-            tap = (2 - p) * 3 + (2 - q)
-            for r in range(2):
-                row = r * TAPS + tap * CH
-                kg_out[p, q, r] = packed[row : row + CH, 0:CH]
-    for tap in range(9):
-        p, q = 2 - tap // 3, 2 - tap % 3
-        for first in range(tap * CH, tap * CH + CH, 8):
-            local = first - tap * CH
-            if first < KEPT:
-                slab = packed[2 * TAPS + first : 2 * TAPS + first + 8]
-            else:
-                slab = jnp.zeros((8, 128), F32)
-                for k in range(3):
-                    row = 3 * KEPT * k + first - KEPT
-                    piece = pltpu.roll(packed[row : row + 8], 32 + 32 * k, 1)
-                    slab = jnp.where(lane8 // 32 == k, piece, slab)
-            kg_out[p, q, 2, local : local + 8] = slab[:, 0:CH]
-    store_k = pltpu.make_async_copy(kg_out, kg_hbm, loc_sem.at[4])
-    store_k.start()
-
-    for copy, sends, _ in halos:
-        pl.when(sends)(copy.wait_send)
-    waiting += [core_copy] + plane_copies + z_copies + fin_copies + blk_copies
+    store_fin = pltpu.make_async_copy(final, fin_hbm, loc_sem.at[7])
+    store_fin.start()
+
+    pl.when(has_down)(next_two.wait_send)
+    pl.when(has_across)(rows_far.wait_send)
+    pl.when(jnp.logical_and(has_down, has_across))(corner_far.wait_send)
+    pl.when(has_up)(corner_core.wait_send)
+    waiting += [core_copy, rows_core] + plane_copies + z_copies + blk_copies
     waiting += spread_copies + pass_copies
     for copy in waiting:
         copy.wait_send()
     store_x.wait()
-    store_k.wait()
+    store_small.wait()
+    store_fin.wait()
+
+
+def unpack_body(
+    out_in, fin_in, small_in, out_hbm, kg_hbm, gain_ref, shift_ref, fin_ref, small_ref, kg, sems
+):
+    load = pltpu.make_async_copy(fin_in, fin_ref, sems.at[4])
+    load.start()
+    load_small = pltpu.make_async_copy(small_in, small_ref, sems.at[5])
+    load_small.start()
+    store = pltpu.make_async_copy(out_in, out_hbm, sems.at[3])
+    store.start()
+    load_small.wait()
+    gain_ref[...] = small_ref[7:8, 0:CH]
+    shift_ref[...] = small_ref[3:4, 0:CH]
+    load.wait()
+    lanes = lax.broadcasted_iota(jnp.int32, (16, 128), 1)
+    stores = []
+    for p in range(3):
+        for q in range(3):
+            tap = ((2 - p) * 3 + 2 - q) * CH
+            for r in range(2):
+                kg[p, q, r] = fin_ref[r * TAPS + tap : r * TAPS + tap + CH].astype(F32)[:, 0:CH]
+            for first in range(tap, tap + CH, 16):
+                if first < KEPT:
+                    slab = fin_ref[2 * TAPS + first : 2 * TAPS + first + 16].astype(F32)
+                else:
+                    slab = None
+                    for k in range(3):
+                        row = MOVED * k + first - KEPT
+                        piece = pltpu.roll(fin_ref[row : row + 16].astype(F32), 32 + 32 * k, 1)
+                        slab = piece if k == 0 else jnp.where(lanes // 32 == k, piece, slab)
+                kg[p, q, 2, first - tap : first - tap + 16] = slab[:, 0:CH]
+        stores.append(pltpu.make_async_copy(kg.at[p], kg_hbm.at[p], sems.at[p]))
+        stores[-1].start()
+    for copy in stores + [store]:
+        copy.wait()
 
 
 def shards(sizes, inputs, out_grads, kernel, norm_gain, norm_shift):
     nb, nz = sizes
     plane = 2 * nb
     share = HALF // plane
-    copies = 5 + 2 * (3 + nz - 1) + 1 + 2 * (plane - 1) + 2 * (nz - 1) + nb - 1 + plane
+    copies = 5 + 2 * (3 + nz - 1) + 1 + 2 * (plane - 1) + (nz - 1) + nb - 1 + plane
     vmem = pltpu.VMEM
-    pad = lambda v: jnp.pad(v, (0, 128 - CH)).reshape(1, 128)
+    in_vmem = pl.BlockSpec(memory_space=pltpu.VMEM)
     any_space = pl.BlockSpec(memory_space=pl.ANY)
-    in_vmem = pl.BlockSpec(memory_space=pltpu.VMEM)
     cells = FRAMES * ROWS
-    out, grad, small = pl.pallas_call(
+    out, final, small = pl.pallas_call(
         functools.partial(body, sizes),
         out_shape=(
             jax.ShapeDtypeStruct((FRAMES, ROWS, CH, COLS), BF16),
-            jax.ShapeDtypeStruct((3, 3, 3, CH, CH), F32),
+            jax.ShapeDtypeStruct((FLAT, 128), BF16),
             jax.ShapeDtypeStruct((8, 128), F32),
         ),
-        in_specs=[any_space] * 3 + [in_vmem] * 2,
-        out_specs=(any_space, any_space, in_vmem),
+        in_specs=[any_space] * 5,
+        out_specs=(any_space,) * 3,
         scratch_shapes=[
+            vmem((1, CH), F32),
+            vmem((1, CH), F32),
+            vmem((FRAMES, ROWS, CH, COLS), BF16),
+            vmem((8, 128), F32),
             vmem((FRAMES, ROWS, CH, COLS), BF16),
             vmem((FRAMES + 2, ROWS + 2, CH, COLS), BF16),
             vmem((3, 3, 3, CH, CH), BF16),
@@ -465,19 +488,15 @@
             vmem((cells, 3 * 128, COLS), BF16),
             vmem((TAPS, 3 * 128), F32),
             vmem((cells, CH, COLS), F32),
-            vmem((FRAMES, ROWS, CH, COLS), BF16),
             vmem((FLAT, 128), F32),
             vmem((HALF, 128), BF16),
             vmem((HALF, 128), BF16),
             vmem((HALF, 128), BF16),
             vmem((plane - 1, share, 128), BF16),
-            vmem((share, 128), F32),
-            vmem((nz, share // nz, 128), F32),
-            vmem((share // nz, 128), F32),
-            vmem((share, 128), F32),
+            vmem((share, 128), BF16),
+            vmem((nz, share, 128), BF16),
             vmem((FLAT, 128), BF16),
             vmem((share, 128), BF16),
-            vmem((3, 3, 3, CH, CH), F32),
             vmem((128, 128), F32),
             vmem((2, 8, 128), F32),
             vmem((2, 4, 8, 128), F32),
@@ -485,15 +504,36 @@
             vmem((2, nz, 8, 128), F32),
             vmem((8, 128), F32),
             vmem((nb, 8, 128), F32),
-            pltpu.SemaphoreType.DMA((5,)),
+            pltpu.SemaphoreType.DMA((8,)),
             pltpu.SemaphoreType.DMA((copies,)),
             pltpu.SemaphoreType.DMA((copies,)),
         ],
         compiler_params=pltpu.CompilerParams(
-            collective_id=0, has_side_effects=True, vmem_limit_bytes=40 * 1024 * 1024
+            collective_id=0, has_side_effects=True, vmem_limit_bytes=60 * 1024 * 1024
         ),
-    )(inputs, out_grads, kernel.transpose(0, 1, 3, 2, 4), pad(norm_gain), pad(norm_shift))
-    return (out, grad.transpose(0, 1, 3, 2, 4), small[7, :CH], small[3, :CH])
+    )(
+        inputs, out_grads, kernel.transpose(0, 1, 3, 2, 4),
+        norm_gain.reshape(1, CH), norm_shift.reshape(1, CH),
+    )
+    out, grad, gain, shift = pl.pallas_call(
+        unpack_body,
+        out_shape=(
+            jax.ShapeDtypeStruct((FRAMES, ROWS, CH, COLS), BF16),
+            jax.ShapeDtypeStruct((3, 3, 3, CH, CH), F32),
+            jax.ShapeDtypeStruct((1, CH), F32),
+            jax.ShapeDtypeStruct((1, CH), F32),
+        ),
+        in_specs=[any_space] * 3,
+        out_specs=(any_space, any_space, in_vmem, in_vmem),
+        scratch_shapes=[
+            vmem((FLAT, 128), BF16),
+            vmem((8, 128), F32),
+            vmem((3, 3, 3, CH, CH), F32),
+            pltpu.SemaphoreType.DMA((6,)),
+        ],
+        compiler_params=pltpu.CompilerParams(vmem_limit_bytes=60 * 1024 * 1024),
+    )(out, final, small)
+    return (out, grad.transpose(0, 1, 3, 2, 4), gain.reshape(CH), shift.reshape(CH))
 
 
 def solution(mesh):

time: 62 us -> 64.5 us (1.040)
  Pallas kernels: 55.1 us -> 63.8 us
  local copies, waits for them, and re-layouts: 6.08 us -> 0 us
    pallas_call x0 -> x1, Pallas kernels: none -> 13.6 us  [shards(): pl.pallas_call(unpack_body, out_shape=(jax.ShapeDtypeStruct((FRAMES, ROWS...]
    pallas_call x1, Pallas kernels: 55.1 us -> 50.2 us  [shards(): pl.pallas_call(functools.partial(body, sizes), out_shape=(jax.ShapeDtypeS...]
    unnamed x8 -> x0, local copies, waits for them, and re-layouts: 4.89 us -> none
    reshape x1 -> x0, local copies, waits for them, and re-layouts: 0.68 us -> none  [shards(): pad = lambda v: jnp.pad(v, (0, 128 - CH)).reshape(1, 128)]
where the time goes in v2:
time: 64.5 us; the launch traced here: 64.4 us
  Pallas kernels  63.8 us (99%)
    pallas_call x1, Pallas kernels, shards(): pl.pallas_call(functools.partial(body, sizes), out_shape=(jax.ShapeDtypeS...  50.2 us
    pallas_call x1, Pallas kernels, shards(): pl.pallas_call(unpack_body, out_shape=(jax.ShapeDtypeStruct((FRAMES, ROWS...  13.6 us

profile of v2, /device:TPU:1, one launch (start us, length us, event | category | flops | bytes accessed | tf_op | source)
XLA Modules:
  0.0 64.4 jit_solution(1354014696760943996)
XLA Ops:
  0.6 50.2 %shard_map.84 = (bf16[4,2,96,256]{3,2,1,0:T(8,128)(2,1)}, bf16[2048,128]{1,0:T(8,128)(2,1)}, f32[8,128]{1,0:T(8,128)}) custom-call(bf16[4,2,96,256]{3,2,1,0:T(8,128)(2,1)} %x_hbm.1, bf16[4,2,96,256]{3,2,1,0:T(8,128)(2,1)} %g_hbm.1, bf16[3,3,3,96,96]{4,3,2,1,0:T(8,128)(2,1)} %bitcast.6, f32[1,96]{1,0:T(1,128)} %bitcast.7, f32[1,96]{1,0:T(1,128)} %bitcast.8), custom_call_target="tpu_custom_call" | custom-call | tf_op jit(solution)/shard_map/pallas_call | solution.py:468
  50.8 13.6 %shard_map.85 = (bf16[4,2,96,256]{3,2,1,0:T(8,128)(2,1)}, f32[3,3,3,96,96]{4,3,2,1,0:T(8,128)}, f32[1,96]{1,0:T(1,128)}, f32[1,96]{1,0:T(1,128)}) custom-call(bf16[4,2,96,256]{3,2,1,0:T(8,128)(2,1)} %get-tuple-element.11.out_in, bf16[2048,128]{1,0:T(8,128)(2,1)} %get-tuple-element.12.fin_in, f32[8,128]{1,0:T(8,128)} %get-tuple-element.13.small_in), custom_call_target="tpu_custom_call" | custom-call | tf_op jit(solution)/shard_map/pallas_call | solution.py:518

commit v3 on v2

--- a/solution.py
+++ b/solution.py
@@ -40,7 +40,7 @@
     out_hbm, fin_hbm, small_hbm,
     gain_ref, shift_ref, outv, small_ref, xv, gp, wv, wst, factor, normed, acts, acc, pre,
     packed, core_send, core_got, plane_send, plane_got, z_send, z_got,
-    final, plane_fin, tmat, st_send, quad_got, st_mid, col_got, blk_send, blk_got,
+    final, plane_fin, tmat, st_send, core_stat, st_mid, tile_got, blk_send, blk_got,
     loc_sem, ssem, rsem,
 ):
     nb, nz = sizes
@@ -56,7 +56,6 @@
     xl, y = b // ny, lax.rem(b, ny)
     flip_c = t + 1 - 2 * c
     flip_x = t + 2 - 4 * xh
-    flip_cx = flip_c + 2 - 4 * xh
     across = lax.rem(t + nt - 1 + 2 * c, nt)
     b_up = lax.rem(b + 1, nb)
     b_down = lax.rem(b + nb - 1, nb)
@@ -99,8 +98,10 @@
     friends = [device for _, device in to_plane]
     far_first = sorted(range(1, nz), key=lambda d: -min(d, nz - d))
     column = [(b, lax.rem(t + 4 * d, nt)) for d in far_first]
-    friends += column
-    friends += [(b, across), (b_up, across), (b_down, across), (b, flip_c), (b, flip_cx)]
+    same_core = [(b, lax.rem(flip_x + 4 * d, nt)) for d in far_first] + column
+    friends += same_core
+    friends += [(b, across), (b_up, across), (b_down, across), (b, flip_c)]
+    same_core.append((b, flip_x))
     for device in friends:
         pl.semaphore_signal(barrier, inc=1, device_id=device, device_id_type=MESH)
 
@@ -134,7 +135,7 @@
             two = two + halved(value * value)
         firsts.append(jnp.sum(one, axis=1, keepdims=True))
         seconds.append(jnp.sum(two, axis=1, keepdims=True))
-    st_send[0] = channel_tile(firsts + seconds)
+    sums = channel_tile(firsts + seconds)
 
     pl.semaphore_wait(barrier, len(friends))
 
@@ -149,44 +150,31 @@
     corner_core = remote(gp.at[late, 2 - c], gp.at[late, 3 * c], (b, flip_c))
 
     def all_sum(tile, at):
-        quad = 2 * xh + c
-        copies = []
-        for k, other in enumerate((flip_c, flip_x, flip_cx)):
-            slot = lax.rem(other, 4)
-            copies.append((
-                remote(st_send.at[at], quad_got.at[at, quad], (b, other)),
-                quad_got.at[at, slot],
-            ))
-        for copy, _ in copies:
-            copy.start()
-        quad_got[at, quad] = tile
-        return copies
-
-    def quad_sum(copies, at):
-        for copy, _ in copies:
-            copy.wait_recv()
-        total = quad_got[at, 0]
-        for k in range(1, 4):
-            total = total + quad_got[at, k]
+        st_send[at] = tile
+        copy = remote(st_send.at[at], core_stat.at[at], (b, flip_c))
+        copy.start()
+        return copy
+
+    def core_sum(copy, at):
+        copy.wait_recv()
+        total = st_send[at] + core_stat[at]
         st_mid[at] = total
-        out = []
-        for device in column:
-            out.append(remote(st_mid.at[at], col_got.at[at, z], device))
+        out = [remote(st_mid.at[at], tile_got.at[at, t // 2], device) for device in same_core]
         for copy in out:
             copy.start()
-        col_got[at, z] = total
+        tile_got[at, t // 2] = total
         return out
 
-    def col_sum(copies, at):
+    def tile_sum(copies, at):
         for copy in copies:
             copy.wait_recv()
-        total = col_got[at, 0]
-        for k in range(1, nz):
-            total = total + col_got[at, k]
+        total = tile_got[at, 0]
+        for k in range(1, 2 * nz):
+            total = total + tile_got[at, k]
         return total
 
     waiting = []
-    stat_copies = all_sum(st_send[0], 0)
+    stat_copy = all_sum(sums, 0)
     pl.when(has_down)(next_two.start)
     pl.when(has_across)(rows_far.start)
     rows_core.start()
@@ -202,8 +190,8 @@
 
     acc[...] = jnp.zeros_like(acc)
     acts[...] = jnp.zeros_like(acts)
-    stat_copies_z = quad_sum(stat_copies, 0)
-    waiting += [copy for copy, _ in stat_copies] + stat_copies_z
+    stat_copies = core_sum(stat_copy, 0)
+    waiting += [stat_copy] + stat_copies
 
     load_w.wait()
     for r in range(3):
@@ -213,7 +201,7 @@
         wst[r * CH : (r + 1) * CH, :] = slab.astype(F32).T.astype(BF16)
 
     number = float(nt * ROWS * COLS * (CH // GROUPS))
-    sums = group_sum(col_sum(stat_copies_z, 0), lane8) / number
+    sums = group_sum(tile_sum(stat_copies, 0), lane8) / number
     center_rows = sums
     square_rows = pltpu.roll(sums, 4, 0)
     spread_rows = lax.rsqrt(square_rows - center_rows * center_rows + EPSILON)
@@ -228,24 +216,8 @@
     vectors = tmat[...].T[0:CH, :]
     gain, shift = vectors[:, 0:1], vectors[:, 1:2]
 
-    for f in range(FRAMES):
-        center, spread = stats[:, f : f + 1], stats[:, 4 + f : 5 + f]
-        for r in range(ROWS):
-            n = f * ROWS + r
-            scaled = (xv[f, r].astype(F32) - center) * spread
-            shaped = scaled * gain + shift
-            logistic = 1.0 / (1.0 + jnp.exp(-shaped))
-            active = shaped * logistic
-            normed[n] = scaled
-            factor[n] = logistic * (1.0 + shaped * (1.0 - logistic))
-            before = jnp.where(col == 0, 0.0, pltpu.roll(active, 1, 1))
-            after = jnp.where(col == COLS - 1, 0.0, pltpu.roll(active, COLS - 1, 1))
-            acts[n, 0:CH] = before.astype(BF16)
-            acts[n, 128 : 128 + CH] = active.astype(BF16)
-            acts[n, 256 : 256 + CH] = after.astype(BF16)
-
-    def kernel_terms(late_frames, edge_rows):
-        for f in range(FRAMES):
+    def kernel_terms(late_frames, edge_rows, frames=range(FRAMES)):
+        for f in frames:
             lo, hi = (max(f, FRAMES), f + 3) if late_frames else (f, min(f + 3, FRAMES))
             if lo >= hi:
                 continue
@@ -264,13 +236,28 @@
                     row = (3 * (lo + k - f) + top - r) * CH
                     acc[row : row + height] += product[k * height : (k + 1) * height]
 
-    load_g.wait()
-    kernel_terms(False, False)
-
     @pl.when(has_up)
     def _():
         next_two.wait_recv()
         corner_core.start()
+
+    load_g.wait()
+    for f in range(FRAMES):
+        center, spread = stats[:, f : f + 1], stats[:, 4 + f : 5 + f]
+        for r in range(ROWS):
+            n = f * ROWS + r
+            scaled = (xv[f, r].astype(F32) - center) * spread
+            shaped = scaled * gain + shift
+            logistic = 1.0 / (1.0 + jnp.exp(-shaped))
+            active = shaped * logistic
+            normed[n] = scaled
+            factor[n] = logistic * (1.0 + shaped * (1.0 - logistic))
+            before = jnp.where(col == 0, 0.0, pltpu.roll(active, 1, 1))
+            after = jnp.where(col == COLS - 1, 0.0, pltpu.roll(active, COLS - 1, 1))
+            acts[n, 0:CH] = before.astype(BF16)
+            acts[n, 128 : 128 + CH] = active.astype(BF16)
+            acts[n, 256 : 256 + CH] = after.astype(BF16)
+        kernel_terms(False, False, (f,))
 
     kernel_terms(True, False)
     rows_core.wait_recv()
@@ -330,8 +317,7 @@
         firsts.append(jnp.sum(one, axis=1, keepdims=True))
         seconds.append(jnp.sum(two, axis=1, keepdims=True))
     tmat[...] = jnp.zeros((128, 128), F32)
-    st_send[1] = channel_tile(firsts + seconds)
-    stat_copies = all_sum(st_send[1], 1)
+    stat_copy = all_sum(channel_tile(firsts + seconds), 1)
 
     for copy in plane_copies:
         copy.wait_recv()
@@ -344,10 +330,10 @@
     for copy in z_copies:
         copy.start()
 
-    stat_copies_z = quad_sum(stat_copies, 1)
-    waiting += [copy for copy, _ in stat_copies] + stat_copies_z
-
-    total = col_sum(stat_copies_z, 1)
+    stat_copies = core_sum(stat_copy, 1)
+    waiting += [stat_copy] + stat_copies
+
+    total = tile_sum(stat_copies, 1)
     means = channel_columns(group_sum(total * gain_rows, lane8) / number)
 
     pairs = total + pltpu.roll(total, 2, 0)
@@ -396,7 +382,7 @@
     store_small = pltpu.make_async_copy(small_ref, small_hbm, loc_sem.at[6])
     store_small.start()
 
-    for copy, (place, _) in zip(spread_copies, from_plane):
+    for copy, (place, _) in reversed(list(zip(spread_copies, from_plane))):
         copy.wait_recv()
         rows = pl.ds(pl.multiple_of(mine + place * share, share), share)
         pass_copies.append(remote(final.at[rows], final.at[rows], (b, flip_c)))
@@ -421,17 +407,21 @@
 
 
 def unpack_body(
-    out_in, fin_in, small_in, out_hbm, kg_hbm, gain_ref, shift_ref, fin_ref, small_ref, kg, sems
+    out_in, fin_in, small_in, out_hbm, kg_hbm, gain_ref, shift_ref,
+    out_ref, fin_ref, small_ref, kg, sems,
 ):
     load = pltpu.make_async_copy(fin_in, fin_ref, sems.at[4])
     load.start()
     load_small = pltpu.make_async_copy(small_in, small_ref, sems.at[5])
     load_small.start()
-    store = pltpu.make_async_copy(out_in, out_hbm, sems.at[3])
-    store.start()
+    load_out = pltpu.make_async_copy(out_in, out_ref, sems.at[6])
+    load_out.start()
     load_small.wait()
     gain_ref[...] = small_ref[7:8, 0:CH]
     shift_ref[...] = small_ref[3:4, 0:CH]
+    load_out.wait()
+    store = pltpu.make_async_copy(out_ref, out_hbm, sems.at[3])
+    store.start()
     load.wait()
     lanes = lax.broadcasted_iota(jnp.int32, (16, 128), 1)
     stores = []
@@ -460,7 +450,7 @@
     nb, nz = sizes
     plane = 2 * nb
     share = HALF // plane
-    copies = 5 + 2 * (3 + nz - 1) + 1 + 2 * (plane - 1) + (nz - 1) + nb - 1 + plane
+    copies = 5 + 2 * (1 + 2 * nz - 1) + 1 + 2 * (plane - 1) + (nz - 1) + nb - 1 + plane
     vmem = pltpu.VMEM
     in_vmem = pl.BlockSpec(memory_space=pltpu.VMEM)
     any_space = pl.BlockSpec(memory_space=pl.ANY)
@@ -499,9 +489,9 @@
             vmem((share, 128), BF16),
             vmem((128, 128), F32),
             vmem((2, 8, 128), F32),
-            vmem((2, 4, 8, 128), F32),
             vmem((2, 8, 128), F32),
-            vmem((2, nz, 8, 128), F32),
+            vmem((2, 8, 128), F32),
+            vmem((2, 2 * nz, 8, 128), F32),
             vmem((8, 128), F32),
             vmem((nb, 8, 128), F32),
             pltpu.SemaphoreType.DMA((8,)),
@@ -526,10 +516,11 @@
         in_specs=[any_space] * 3,
         out_specs=(any_space, any_space, in_vmem, in_vmem),
         scratch_shapes=[
+            vmem((FRAMES, ROWS, CH, COLS), BF16),
             vmem((FLAT, 128), BF16),
             vmem((8, 128), F32),
             vmem((3, 3, 3, CH, CH), F32),
-            pltpu.SemaphoreType.DMA((6,)),
+            pltpu.SemaphoreType.DMA((7,)),
         ],
         compiler_params=pltpu.CompilerParams(vmem_limit_bytes=60 * 1024 * 1024),
     )(out, final, small)

time: 64.5 us -> 55.1 us (0.85)
  Pallas kernels: 63.8 us -> 54.4 us
    pallas_call x1, Pallas kernels: 13.6 us -> 2.92 us  [shards(): pl.pallas_call(unpack_body, out_shape=(jax.ShapeDtypeStruct((FRAMES, ROWS...]
    pallas_call x1, Pallas kernels: 50.2 us -> 51.4 us  [shards(): pl.pallas_call(functools.partial(body, sizes), out_shape=(jax.ShapeDtypeS...]
where the time goes in v3:
time: 55.1 us; the launch traced here: 55 us
  Pallas kernels  54.4 us (99%)
  between operations  0.64 us (1%)
    pallas_call x1, Pallas kernels, shards(): pl.pallas_call(functools.partial(body, sizes), out_shape=(jax.ShapeDtypeS...  51.4 us
    pallas_call x1, Pallas kernels, shards(): pl.pallas_call(unpack_body, out_shape=(jax.ShapeDtypeStruct((FRAMES, ROWS...  2.92 us

profile of v3, /device:TPU:1, one launch (start us, length us, event | category | flops | bytes accessed | tf_op | source)
XLA Modules:
  0.0 55.0 jit_solution(7613614983932478675)
XLA Ops:
  0.6 51.4 %shard_map.84 = (bf16[4,2,96,256]{3,2,1,0:T(8,128)(2,1)}, bf16[2048,128]{1,0:T(8,128)(2,1)}, f32[8,128]{1,0:T(8,128)}) custom-call(bf16[4,2,96,256]{3,2,1,0:T(8,128)(2,1)} %x_hbm.1, bf16[4,2,96,256]{3,2,1,0:T(8,128)(2,1)} %g_hbm.1, bf16[3,3,3,96,96]{4,3,2,1,0:T(8,128)(2,1)} %bitcast.6, f32[1,96]{1,0:T(1,128)} %bitcast.7, f32[1,96]{1,0:T(1,128)} %bitcast.8), custom_call_target="tpu_custom_call" | custom-call | tf_op jit(solution)/shard_map/pallas_call | solution.py:458
  52.1 2.9 %shard_map.85 = (bf16[4,2,96,256]{3,2,1,0:T(8,128)(2,1)}, f32[3,3,3,96,96]{4,3,2,1,0:T(8,128)}, f32[1,96]{1,0:T(1,128)}, f32[1,96]{1,0:T(1,128)}) custom-call(bf16[4,2,96,256]{3,2,1,0:T(8,128)(2,1)} %get-tuple-element.11.out_in, bf16[2048,128]{1,0:T(8,128)(2,1)} %get-tuple-element.12.fin_in, f32[8,128]{1,0:T(8,128)} %get-tuple-element.13.small_in), custom_call_target="tpu_custom_call" | custom-call | tf_op jit(solution)/shard_map/pallas_call | solution.py:508

commit v4 on v2

--- a/solution.py
+++ b/solution.py
@@ -190,7 +190,6 @@
     pl.when(has_down)(next_two.start)
     pl.when(has_across)(rows_far.start)
     rows_core.start()
-    pl.when(jnp.logical_and(has_down, has_across))(corner_far.start)
 
     @pl.when(jnp.logical_not(has_across))
     def _():
@@ -203,6 +202,7 @@
     acc[...] = jnp.zeros_like(acc)
     acts[...] = jnp.zeros_like(acts)
     stat_copies_z = quad_sum(stat_copies, 0)
+    pl.when(jnp.logical_and(has_down, has_across))(corner_far.start)
     waiting += [copy for copy, _ in stat_copies] + stat_copies_z
 
     load_w.wait()
@@ -228,24 +228,8 @@
     vectors = tmat[...].T[0:CH, :]
     gain, shift = vectors[:, 0:1], vectors[:, 1:2]
 
-    for f in range(FRAMES):
-        center, spread = stats[:, f : f + 1], stats[:, 4 + f : 5 + f]
-        for r in range(ROWS):
-            n = f * ROWS + r
-            scaled = (xv[f, r].astype(F32) - center) * spread
-            shaped = scaled * gain + shift
-            logistic = 1.0 / (1.0 + jnp.exp(-shaped))
-            active = shaped * logistic
-            normed[n] = scaled
-            factor[n] = logistic * (1.0 + shaped * (1.0 - logistic))
-            before = jnp.where(col == 0, 0.0, pltpu.roll(active, 1, 1))
-            after = jnp.where(col == COLS - 1, 0.0, pltpu.roll(active, COLS - 1, 1))
-            acts[n, 0:CH] = before.astype(BF16)
-            acts[n, 128 : 128 + CH] = active.astype(BF16)
-            acts[n, 256 : 256 + CH] = after.astype(BF16)
-
-    def kernel_terms(late_frames, edge_rows):
-        for f in range(FRAMES):
+    def kernel_terms(late_frames, edge_rows, frames=range(FRAMES)):
+        for f in frames:
             lo, hi = (max(f, FRAMES), f + 3) if late_frames else (f, min(f + 3, FRAMES))
             if lo >= hi:
                 continue
@@ -264,13 +248,28 @@
                     row = (3 * (lo + k - f) + top - r) * CH
                     acc[row : row + height] += product[k * height : (k + 1) * height]
 
-    load_g.wait()
-    kernel_terms(False, False)
-
     @pl.when(has_up)
     def _():
         next_two.wait_recv()
         corner_core.start()
+
+    load_g.wait()
+    for f in range(FRAMES):
+        center, spread = stats[:, f : f + 1], stats[:, 4 + f : 5 + f]
+        for r in range(ROWS):
+            n = f * ROWS + r
+            scaled = (xv[f, r].astype(F32) - center) * spread
+            shaped = scaled * gain + shift
+            logistic = 1.0 / (1.0 + jnp.exp(-shaped))
+            active = shaped * logistic
+            normed[n] = scaled
+            factor[n] = logistic * (1.0 + shaped * (1.0 - logistic))
+            before = jnp.where(col == 0, 0.0, pltpu.roll(active, 1, 1))
+            after = jnp.where(col == COLS - 1, 0.0, pltpu.roll(active, COLS - 1, 1))
+            acts[n, 0:CH] = before.astype(BF16)
+            acts[n, 128 : 128 + CH] = active.astype(BF16)
+            acts[n, 256 : 256 + CH] = after.astype(BF16)
+        kernel_terms(False, False, (f,))
 
     kernel_terms(True, False)
     rows_core.wait_recv()
@@ -297,8 +296,7 @@
     core_copy = remote(core_send, core_got, (b, flip_c))
     core_copy.start()
 
-    @pl.loop(0, FRAMES * ROWS)
-    def _(n):
+    def act_grad(n):
         f, r = n // ROWS, lax.rem(n, ROWS)
         window = gp[pl.ds(f, 3), pl.ds(r, 3)].reshape(TAPS, COLS)
         product = jnp.dot(wst[...], window, preferred_element_type=F32)
@@ -308,6 +306,7 @@
         before = jnp.where(col == 0, 0.0, before)
         pre[n] = (after + product[CH : 2 * CH] + before) * factor[n]
 
+    pl.loop(0, 4)(act_grad)
     core_copy.wait_recv()
     chip = packed[pl.ds(mine, HALF)] + core_got[...].astype(F32)
     packed[pl.ds(mine, HALF)] = chip
@@ -318,6 +317,8 @@
         plane_copies.append(remote(plane_send.at[rows], plane_got.at[k], device))
     for copy in plane_copies:
         copy.start()
+
+    pl.loop(4, FRAMES * ROWS)(act_grad)
 
     firsts, seconds = [], []
     for f in range(FRAMES):
@@ -346,20 +347,6 @@
 
     stat_copies_z = quad_sum(stat_copies, 1)
     waiting += [copy for copy, _ in stat_copies] + stat_copies_z
-
-    total = col_sum(stat_copies_z, 1)
-    means = channel_columns(group_sum(total * gain_rows, lane8) / number)
-
-    pairs = total + pltpu.roll(total, 2, 0)
-    pairs = pairs + pltpu.roll(pairs, 1, 0)
-    blk_send[...] = pairs
-    blk_got[b] = pairs
-    blk_copies = []
-    for d in range(1, nb):
-        block = lax.rem(b + d, nb)
-        blk_copies.append(remote(blk_send, blk_got.at[b], (block, t)))
-    for copy in blk_copies:
-        copy.start()
 
     for copy in z_copies:
         copy.wait_recv()
@@ -377,6 +364,20 @@
     pass_copies = [remote(plane_fin, final.at[own_rows], (b, flip_c))]
     pass_copies[0].start()
 
+    total = col_sum(stat_copies_z, 1)
+    means = channel_columns(group_sum(total * gain_rows, lane8) / number)
+
+    pairs = total + pltpu.roll(total, 2, 0)
+    pairs = pairs + pltpu.roll(pairs, 1, 0)
+    blk_send[...] = pairs
+    blk_got[b] = pairs
+    blk_copies = []
+    for d in range(1, nb):
+        block = lax.rem(b + d, nb)
+        blk_copies.append(remote(blk_send, blk_got.at[b], (block, t)))
+    for copy in blk_copies:
+        copy.start()
+
     for f in range(FRAMES):
         spread = stats[:, 4 + f : 5 + f]
         m1, m2 = means[:, f : f + 1], means[:, 4 + f : 5 + f]
@@ -387,6 +388,11 @@
     store_x = pltpu.make_async_copy(outv, out_hbm, loc_sem.at[5])
     store_x.start()
 
+    for copy, (place, _) in reversed(list(zip(spread_copies, from_plane))):
+        copy.wait_recv()
+        rows = pl.ds(pl.multiple_of(mine + place * share, share), share)
+        pass_copies.append(remote(final.at[rows], final.at[rows], (b, flip_c)))
+        pass_copies[-1].start()
     for copy in blk_copies:
         copy.wait_recv()
     total = blk_got[0]
@@ -396,11 +402,6 @@
     store_small = pltpu.make_async_copy(small_ref, small_hbm, loc_sem.at[6])
     store_small.start()
 
-    for copy, (place, _) in zip(spread_copies, from_plane):
-        copy.wait_recv()
-        rows = pl.ds(pl.multiple_of(mine + place * share, share), share)
-        pass_copies.append(remote(final.at[rows], final.at[rows], (b, flip_c)))
-        pass_copies[-1].start()
     for copy in pass_copies:
         copy.wait_recv()
 
@@ -421,38 +422,52 @@
 
 
 def unpack_body(
-    out_in, fin_in, small_in, out_hbm, kg_hbm, gain_ref, shift_ref, fin_ref, small_ref, kg, sems
+    out_in, fin_in, small_in, out_hbm, kg_hbm, gain_ref, shift_ref,
+    out_ref, fin_ref, small_ref, kg, sems,
 ):
-    load = pltpu.make_async_copy(fin_in, fin_ref, sems.at[4])
-    load.start()
-    load_small = pltpu.make_async_copy(small_in, small_ref, sems.at[5])
+    bounds = (0, TAPS, 2 * TAPS, FLAT)
+    loads = []
+    for k in range(3):
+        rows = pl.ds(bounds[k], bounds[k + 1] - bounds[k])
+        loads.append(pltpu.make_async_copy(fin_in.at[rows], fin_ref.at[rows], sems.at[k]))
+        loads[k].start()
+    load_out = pltpu.make_async_copy(out_in, out_ref, sems.at[3])
+    load_out.start()
+    load_small = pltpu.make_async_copy(small_in, small_ref, sems.at[4])
     load_small.start()
-    store = pltpu.make_async_copy(out_in, out_hbm, sems.at[3])
-    store.start()
+    lanes = lax.broadcasted_iota(jnp.int32, (16, 128), 1)
+    stores = []
+    for r in range(3):
+        loads[r].wait()
+        for p in range(3):
+            for q in range(3):
+                tap = ((2 - p) * 3 + 2 - q) * CH
+                if r < 2:
+                    slab = fin_ref[r * TAPS + tap : r * TAPS + tap + CH].astype(F32)
+                    kg[p, q, r] = slab[:, 0:CH]
+                    continue
+                for first in range(tap, tap + CH, 16):
+                    if first < KEPT:
+                        slab = fin_ref[2 * TAPS + first : 2 * TAPS + first + 16].astype(F32)
+                    else:
+                        slab = None
+                        for k in range(3):
+                            row = MOVED * k + first - KEPT
+                            piece = fin_ref[row : row + 16].astype(F32)
+                            piece = pltpu.roll(piece, 32 + 32 * k, 1)
+                            slab = piece if k == 0 else jnp.where(lanes // 32 == k, piece, slab)
+                    kg[p, q, 2, first - tap : first - tap + 16] = slab[:, 0:CH]
+        store = pltpu.make_async_copy(kg.at[:, :, r], kg_hbm.at[:, :, r], sems.at[5 + r])
+        store.start()
+        stores.append(store)
+        if r == 0:
+            load_out.wait()
+            stores.append(pltpu.make_async_copy(out_ref, out_hbm, sems.at[8]))
+            stores[-1].start()
     load_small.wait()
     gain_ref[...] = small_ref[7:8, 0:CH]
     shift_ref[...] = small_ref[3:4, 0:CH]
-    load.wait()
-    lanes = lax.broadcasted_iota(jnp.int32, (16, 128), 1)
-    stores = []
-    for p in range(3):
-        for q in range(3):
-            tap = ((2 - p) * 3 + 2 - q) * CH
-            for r in range(2):
-                kg[p, q, r] = fin_ref[r * TAPS + tap : r * TAPS + tap + CH].astype(F32)[:, 0:CH]
-            for first in range(tap, tap + CH, 16):
-                if first < KEPT:
-                    slab = fin_ref[2 * TAPS + first : 2 * TAPS + first + 16].astype(F32)
-                else:
-                    slab = None
-                    for k in range(3):
-                        row = MOVED * k + first - KEPT
-                        piece = pltpu.roll(fin_ref[row : row + 16].astype(F32), 32 + 32 * k, 1)
-                        slab = piece if k == 0 else jnp.where(lanes // 32 == k, piece, slab)
-                kg[p, q, 2, first - tap : first - tap + 16] = slab[:, 0:CH]
-        stores.append(pltpu.make_async_copy(kg.at[p], kg_hbm.at[p], sems.at[p]))
-        stores[-1].start()
-    for copy in stores + [store]:
+    for copy in stores:
         copy.wait()
 
 
@@ -526,10 +541,11 @@
         in_specs=[any_space] * 3,
         out_specs=(any_space, any_space, in_vmem, in_vmem),
         scratch_shapes=[
+            vmem((FRAMES, ROWS, CH, COLS), BF16),
             vmem((FLAT, 128), BF16),
             vmem((8, 128), F32),
             vmem((3, 3, 3, CH, CH), F32),
-            pltpu.SemaphoreType.DMA((6,)),
+            pltpu.SemaphoreType.DMA((9,)),
         ],
         compiler_params=pltpu.CompilerParams(vmem_limit_bytes=60 * 1024 * 1024),
     )(out, final, small)

time: 64.5 us -> 49.2 us (0.76)
  Pallas kernels: 63.8 us -> 48.4 us
    pallas_call x1, Pallas kernels: 13.6 us -> 2.89 us  [shards(): pl.pallas_call(unpack_body, out_shape=(jax.ShapeDtypeStruct((FRAMES, ROWS...]
    pallas_call x1, Pallas kernels: 50.2 us -> 45.5 us  [shards(): pl.pallas_call(functools.partial(body, sizes), out_shape=(jax.ShapeDtypeS...]
where the time goes in v4:
time: 49.2 us; the launch traced here: 49.1 us
  Pallas kernels  48.4 us (98%)
  between operations  0.64 us (1%)
    pallas_call x1, Pallas kernels, shards(): pl.pallas_call(functools.partial(body, sizes), out_shape=(jax.ShapeDtypeS...  45.5 us
    pallas_call x1, Pallas kernels, shards(): pl.pallas_call(unpack_body, out_shape=(jax.ShapeDtypeStruct((FRAMES, ROWS...  2.89 us

profile of v4, /device:TPU:1, one launch (start us, length us, event | category | flops | bytes accessed | tf_op | source)
XLA Modules:
  0.0 49.1 jit_solution(12643628201242094804)
XLA Ops:
  0.6 45.5 %shard_map.84 = (bf16[4,2,96,256]{3,2,1,0:T(8,128)(2,1)}, bf16[2048,128]{1,0:T(8,128)(2,1)}, f32[8,128]{1,0:T(8,128)}) custom-call(bf16[4,2,96,256]{3,2,1,0:T(8,128)(2,1)} %x_hbm.1, bf16[4,2,96,256]{3,2,1,0:T(8,128)(2,1)} %g_hbm.1, bf16[3,3,3,96,96]{4,3,2,1,0:T(8,128)(2,1)} %bitcast.6, f32[1,96]{1,0:T(1,128)} %bitcast.7, f32[1,96]{1,0:T(1,128)} %bitcast.8), custom_call_target="tpu_custom_call" | custom-call | tf_op jit(solution)/shard_map/pallas_call | solution.py:483
  46.2 2.9 %shard_map.85 = (bf16[4,2,96,256]{3,2,1,0:T(8,128)(2,1)}, f32[3,3,3,96,96]{4,3,2,1,0:T(8,128)}, f32[1,96]{1,0:T(1,128)}, f32[1,96]{1,0:T(1,128)}) custom-call(bf16[4,2,96,256]{3,2,1,0:T(8,128)(2,1)} %get-tuple-element.11.out_in, bf16[2048,128]{1,0:T(8,128)(2,1)} %get-tuple-element.12.fin_in, f32[8,128]{1,0:T(8,128)} %get-tuple-element.13.small_in), custom_call_target="tpu_custom_call" | custom-call | tf_op jit(solution)/shard_map/pallas_call | solution.py:533

commit v5 on v4

--- a/solution.py
+++ b/solution.py
@@ -84,6 +84,17 @@
     to_plane = [plane_at(dx, dy) for dx, dy in steps]
     from_plane = [plane_at((4 - dx) % 4, (ny - dy) % ny) for dx, dy in steps]
 
+    barrier = pltpu.get_barrier_semaphore()
+    far_first = sorted(range(1, nz), key=lambda d: -min(d, nz - d))
+    column = [(b, lax.rem(t + 4 * d, nt)) for d in far_first]
+    hops = [(min(dx, 4 - dx) + min(dy, ny - dy), place[1]) for (dx, dy), place in zip(steps, to_plane)]
+    hops += [(min(d, nz - d), device) for d, device in zip(far_first, column)]
+    hops.sort(key=lambda pair: -pair[0])
+    friends = [device for _, device in hops]
+    friends += [(b, across), (b_up, across), (b_down, across), (b, flip_c), (b, flip_cx)]
+    for device in friends:
+        pl.semaphore_signal(barrier, inc=1, device_id=device, device_id_type=MESH)
+
     load_x = pltpu.make_async_copy(x_hbm, xv, loc_sem.at[0])
     load_g = pltpu.make_async_copy(g_hbm, gp.at[pl.ds(0, FRAMES), pl.ds(1, ROWS)], loc_sem.at[1])
     load_w = pltpu.make_async_copy(w_hbm, wv, loc_sem.at[2])
@@ -94,15 +105,6 @@
     load_gain.start()
     load_shift.start()
     load_w.start()
-
-    barrier = pltpu.get_barrier_semaphore()
-    friends = [device for _, device in to_plane]
-    far_first = sorted(range(1, nz), key=lambda d: -min(d, nz - d))
-    column = [(b, lax.rem(t + 4 * d, nt)) for d in far_first]
-    friends += column
-    friends += [(b, across), (b_up, across), (b_down, across), (b, flip_c), (b, flip_cx)]
-    for device in friends:
-        pl.semaphore_signal(barrier, inc=1, device_id=device, device_id_type=MESH)
 
     lane = lax.broadcasted_iota(jnp.int32, (CH, 128), 1)
     lane8 = lax.broadcasted_iota(jnp.int32, (8, 128), 1)
@@ -388,11 +390,23 @@
     store_x = pltpu.make_async_copy(outv, out_hbm, loc_sem.at[5])
     store_x.start()
 
+    pl.when(has_down)(next_two.wait_send)
+    pl.when(has_across)(rows_far.wait_send)
+    pl.when(jnp.logical_and(has_down, has_across))(corner_far.wait_send)
+    pl.when(has_up)(corner_core.wait_send)
+    waiting += [core_copy, rows_core] + plane_copies + z_copies
+    for copy in waiting:
+        copy.wait_send()
+
     for copy, (place, _) in reversed(list(zip(spread_copies, from_plane))):
         copy.wait_recv()
         rows = pl.ds(pl.multiple_of(mine + place * share, share), share)
         pass_copies.append(remote(final.at[rows], final.at[rows], (b, flip_c)))
         pass_copies[-1].start()
+    store_mine = pltpu.make_async_copy(
+        final.at[pl.ds(mine, HALF)], fin_hbm.at[pl.ds(mine, HALF)], loc_sem.at[7]
+    )
+    store_mine.start()
     for copy in blk_copies:
         copy.wait_recv()
     total = blk_got[0]
@@ -405,25 +419,22 @@
     for copy in pass_copies:
         copy.wait_recv()
 
-    store_fin = pltpu.make_async_copy(final, fin_hbm, loc_sem.at[7])
-    store_fin.start()
-
-    pl.when(has_down)(next_two.wait_send)
-    pl.when(has_across)(rows_far.wait_send)
-    pl.when(jnp.logical_and(has_down, has_across))(corner_far.wait_send)
-    pl.when(has_up)(corner_core.wait_send)
-    waiting += [core_copy, rows_core] + plane_copies + z_copies + blk_copies
-    waiting += spread_copies + pass_copies
-    for copy in waiting:
+    store_theirs = pltpu.make_async_copy(
+        final.at[pl.ds(theirs, HALF)], fin_hbm.at[pl.ds(theirs, HALF)], loc_sem.at[8]
+    )
+    store_theirs.start()
+
+    for copy in blk_copies + spread_copies + pass_copies:
         copy.wait_send()
     store_x.wait()
     store_small.wait()
-    store_fin.wait()
+    store_mine.wait()
+    store_theirs.wait()
 
 
 def unpack_body(
-    out_in, fin_in, small_in, out_hbm, kg_hbm, gain_ref, shift_ref,
-    out_ref, fin_ref, small_ref, kg, sems,
+    out_in, fin_in, small_in, out_hbm, kg_hbm, gain_hbm, shift_hbm,
+    out_ref, fin_ref, small_ref, vectors, kg, sems,
 ):
     bounds = (0, TAPS, 2 * TAPS, FLAT)
     loads = []
@@ -462,11 +473,17 @@
         stores.append(store)
         if r == 0:
             load_out.wait()
-            stores.append(pltpu.make_async_copy(out_ref, out_hbm, sems.at[8]))
-            stores[-1].start()
-    load_small.wait()
-    gain_ref[...] = small_ref[7:8, 0:CH]
-    shift_ref[...] = small_ref[3:4, 0:CH]
+            load_small.wait()
+            vectors[0, 0:1] = small_ref[7:8, 0:CH]
+            vectors[1, 0:1] = small_ref[3:4, 0:CH]
+            others = [
+                pltpu.make_async_copy(out_ref, out_hbm, sems.at[8]),
+                pltpu.make_async_copy(vectors.at[0, pl.ds(0, 1)], gain_hbm, sems.at[9]),
+                pltpu.make_async_copy(vectors.at[1, pl.ds(0, 1)], shift_hbm, sems.at[10]),
+            ]
+            for copy in others:
+                copy.start()
+            stores += others
     for copy in stores:
         copy.wait()
 
@@ -477,7 +494,6 @@
     share = HALF // plane
     copies = 5 + 2 * (3 + nz - 1) + 1 + 2 * (plane - 1) + (nz - 1) + nb - 1 + plane
     vmem = pltpu.VMEM
-    in_vmem = pl.BlockSpec(memory_space=pltpu.VMEM)
     any_space = pl.BlockSpec(memory_space=pl.ANY)
     cells = FRAMES * ROWS
     out, final, small = pl.pallas_call(
@@ -519,7 +535,7 @@
             vmem((2, nz, 8, 128), F32),
             vmem((8, 128), F32),
             vmem((nb, 8, 128), F32),
-            pltpu.SemaphoreType.DMA((8,)),
+            pltpu.SemaphoreType.DMA((9,)),
             pltpu.SemaphoreType.DMA((copies,)),
             pltpu.SemaphoreType.DMA((copies,)),
         ],
@@ -539,13 +555,14 @@
             jax.ShapeDtypeStruct((1, CH), F32),
         ),
         in_specs=[any_space] * 3,
-        out_specs=(any_space, any_space, in_vmem, in_vmem),
+        out_specs=(any_space,) * 4,
         scratch_shapes=[
             vmem((FRAMES, ROWS, CH, COLS), BF16),
             vmem((FLAT, 128), BF16),
             vmem((8, 128), F32),
+            vmem((2, 8, CH), F32),
             vmem((3, 3, 3, CH, CH), F32),
-            pltpu.SemaphoreType.DMA((9,)),
+            pltpu.SemaphoreType.DMA((11,)),
         ],
         compiler_params=pltpu.CompilerParams(vmem_limit_bytes=60 * 1024 * 1024),
     )(out, final, small)

time: 49.2 us -> 48.5 us (0.986)
  Pallas kernels: 48.4 us -> 47.8 us
where the time goes in v5:
time: 48.5 us; the launch traced here: 48.4 us
  Pallas kernels  47.8 us (99%)
  between operations  0.64 us (1%)
    pallas_call x1, Pallas kernels, shards(): pl.pallas_call(functools.partial(body, sizes), out_shape=(jax.ShapeDtypeS...  45.4 us
    pallas_call x1, Pallas kernels, shards(): pl.pallas_call(unpack_body, out_shape=(jax.ShapeDtypeStruct((FRAMES, ROWS...  2.4 us

profile of v5, /device:TPU:1, one launch (start us, length us, event | category | flops | bytes accessed | tf_op | source)
XLA Modules:
  0.0 48.4 jit_solution(18116460901184779740)
XLA Ops:
  0.6 45.4 %shard_map.84 = (bf16[4,2,96,256]{3,2,1,0:T(8,128)(2,1)}, bf16[2048,128]{1,0:T(8,128)(2,1)}, f32[8,128]{1,0:T(8,128)}) custom-call(bf16[4,2,96,256]{3,2,1,0:T(8,128)(2,1)} %x_hbm.1, bf16[4,2,96,256]{3,2,1,0:T(8,128)(2,1)} %g_hbm.1, bf16[3,3,3,96,96]{4,3,2,1,0:T(8,128)(2,1)} %bitcast.6, f32[1,96]{1,0:T(1,128)} %bitcast.7, f32[1,96]{1,0:T(1,128)} %bitcast.8), custom_call_target="tpu_custom_call" | custom-call | tf_op jit(solution)/shard_map/pallas_call | solution.py:499
  46.0 2.4 %shard_map.85 = (bf16[4,2,96,256]{3,2,1,0:T(8,128)(2,1)}, f32[3,3,3,96,96]{4,3,2,1,0:T(8,128)}, f32[1,96]{1,0:T(1,128)}, f32[1,96]{1,0:T(1,128)}) custom-call(bf16[4,2,96,256]{3,2,1,0:T(8,128)(2,1)} %get-tuple-element.11.out_in, bf16[2048,128]{1,0:T(8,128)(2,1)} %get-tuple-element.12.fin_in, f32[8,128]{1,0:T(8,128)} %get-tuple-element.13.small_in), custom_call_target="tpu_custom_call" | custom-call | tf_op jit(solution)/shard_map/pallas_call | solution.py:549

commit v6 on v5

--- a/solution.py
+++ b/solution.py
@@ -214,14 +214,7 @@
         )
         wst[r * CH : (r + 1) * CH, :] = slab.astype(F32).T.astype(BF16)
 
-    number = float(nt * ROWS * COLS * (CH // GROUPS))
-    sums = group_sum(col_sum(stat_copies_z, 0), lane8) / number
-    center_rows = sums
-    square_rows = pltpu.roll(sums, 4, 0)
-    spread_rows = lax.rsqrt(square_rows - center_rows * center_rows + EPSILON)
-    both = jnp.where(row8 < 4, center_rows, pltpu.roll(spread_rows, 4, 0))
     tmat[...] = jnp.zeros((128, 128), F32)
-    stats = channel_columns(both)
     load_gain.wait()
     load_shift.wait()
     tmat[0:1, 0:CH] = gain_ref[...]
@@ -229,26 +222,32 @@
     gain_rows = jnp.broadcast_to(tmat[0:1, :], (8, 128))
     vectors = tmat[...].T[0:CH, :]
     gain, shift = vectors[:, 0:1], vectors[:, 1:2]
+    number = float(nt * ROWS * COLS * (CH // GROUPS))
+    sums = group_sum(col_sum(stat_copies_z, 0), lane8) / number
+    center_rows = sums
+    square_rows = pltpu.roll(sums, 4, 0)
+    spread_rows = lax.rsqrt(square_rows - center_rows * center_rows + EPSILON)
+    both = jnp.where(row8 < 4, center_rows, pltpu.roll(spread_rows, 4, 0))
+    stats = channel_columns(both)
 
     def kernel_terms(late_frames, edge_rows, frames=range(FRAMES)):
         for f in frames:
             lo, hi = (max(f, FRAMES), f + 3) if late_frames else (f, min(f + 3, FRAMES))
             if lo >= hi:
                 continue
-            for r in range(ROWS):
-                if edge_rows:
-                    top, rows = 3 * r, 1
-                else:
-                    top, rows = 1, 2
-                window = gp[lo:hi, top : top + rows].reshape((hi - lo) * rows * CH, COLS)
+            for top, r_lo, r_hi in ((0, 0, 1), (3, 1, 2)) if edge_rows else ((1, 0, 2),):
+                rows = r_hi - r_lo
+                height = rows * CH
+                window = gp[lo:hi, top : top + rows].reshape((hi - lo) * height, COLS)
+                both = acts[f * ROWS + r_lo : f * ROWS + r_hi].reshape(rows * 384, COLS)
                 product = lax.dot_general(
-                    window, acts[f * ROWS + r], (((1,), (1,)), ((), ())),
-                    preferred_element_type=F32,
+                    window, both, (((1,), (1,)), ((), ())), preferred_element_type=F32
                 )
-                height = rows * CH
-                for k in range(hi - lo):
-                    row = (3 * (lo + k - f) + top - r) * CH
-                    acc[row : row + height] += product[k * height : (k + 1) * height]
+                for r in range(r_lo, r_hi):
+                    term = product[:, (r - r_lo) * 384 : (r - r_lo + 1) * 384]
+                    for k in range(hi - lo):
+                        row = (3 * (lo + k - f) + top - r) * CH
+                        acc[row : row + height] += term[k * height : (k + 1) * height]
 
     @pl.when(has_up)
     def _():
@@ -299,7 +298,7 @@
     core_copy.start()
 
     def act_grad(n):
-        f, r = n // ROWS, lax.rem(n, ROWS)
+        f, r = n // ROWS, n % ROWS
         window = gp[pl.ds(f, 3), pl.ds(r, 3)].reshape(TAPS, COLS)
         product = jnp.dot(wst[...], window, preferred_element_type=F32)
         after = pltpu.roll(product[0:CH], COLS - 1, 1)
@@ -308,7 +307,6 @@
         before = jnp.where(col == 0, 0.0, before)
         pre[n] = (after + product[CH : 2 * CH] + before) * factor[n]
 
-    pl.loop(0, 4)(act_grad)
     core_copy.wait_recv()
     chip = packed[pl.ds(mine, HALF)] + core_got[...].astype(F32)
     packed[pl.ds(mine, HALF)] = chip
@@ -320,7 +318,8 @@
     for copy in plane_copies:
         copy.start()
 
-    pl.loop(4, FRAMES * ROWS)(act_grad)
+    for n in range(FRAMES * ROWS):
+        act_grad(n)
 
     firsts, seconds = [], []
     for f in range(FRAMES):

time: 48.5 us -> 48.5 us (level)
  no operation moved by 1% of the time
where the time goes in v6:
time: 48.5 us; the launch traced here: 48.3 us
  Pallas kernels  47.7 us (98%)
  between operations  0.64 us (1%)
    pallas_call x1, Pallas kernels, shards(): pl.pallas_call(functools.partial(body, sizes), out_shape=(jax.ShapeDtypeS...  45.3 us
    pallas_call x1, Pallas kernels, shards(): pl.pallas_call(unpack_body, out_shape=(jax.ShapeDtypeStruct((FRAMES, ROWS...  2.4 us

profile of v6, /device:TPU:1, one launch (start us, length us, event | category | flops | bytes accessed | tf_op | source)
XLA Modules:
  0.0 48.3 jit_solution(17684952471955576861)
XLA Ops:
  0.6 45.3 %shard_map.84 = (bf16[4,2,96,256]{3,2,1,0:T(8,128)(2,1)}, bf16[2048,128]{1,0:T(8,128)(2,1)}, f32[8,128]{1,0:T(8,128)}) custom-call(bf16[4,2,96,256]{3,2,1,0:T(8,128)(2,1)} %x_hbm.1, bf16[4,2,96,256]{3,2,1,0:T(8,128)(2,1)} %g_hbm.1, bf16[3,3,3,96,96]{4,3,2,1,0:T(8,128)(2,1)} %bitcast.6, f32[1,96]{1,0:T(1,128)} %bitcast.7, f32[1,96]{1,0:T(1,128)} %bitcast.8), custom_call_target="tpu_custom_call" | custom-call | tf_op jit(solution)/shard_map/pallas_call | solution.py:498
  45.9 2.4 %shard_map.85 = (bf16[4,2,96,256]{3,2,1,0:T(8,128)(2,1)}, f32[3,3,3,96,96]{4,3,2,1,0:T(8,128)}, f32[1,96]{1,0:T(1,128)}, f32[1,96]{1,0:T(1,128)}) custom-call(bf16[4,2,96,256]{3,2,1,0:T(8,128)(2,1)} %get-tuple-element.11.out_in, bf16[2048,128]{1,0:T(8,128)(2,1)} %get-tuple-element.12.fin_in, f32[8,128]{1,0:T(8,128)} %get-tuple-element.13.small_in), custom_call_target="tpu_custom_call" | custom-call | tf_op jit(solution)/shard_map/pallas_call | solution.py:548
